TPU v7x, 512 devices: a whole 4x4x16 slice. The times are simulated.
512 devices in a mesh: ctx: 32 (over x, y, core), row: 16 (over z).
Axes of the slice: x: 4, y: 4, z: 16, core: 2. Of those that a mesh axis runs over, the one named last changes fastest.
Arguments:
- queries: bfloat16 [64, 8192], P('row'), may hold values from -100 to 100
- shared_prefix_cache: bfloat16 [2, 131072, 1024], P(None, ('ctx', 'row')), may hold values from -6 to 6
- row_suffix_cache: bfloat16 [2, 64, 1024, 1024], P(None, 'row', 'ctx'), may hold values from -9 to 9
- row_suffix_length: int32 [64], P('row'), may hold values from 1 to 1024, as said below
- row_adapter_index: int32 [64, 1], P('row'), may hold values from 0 to 15; in each aligned block of 4 rows (0 to 3, 4 to 7, ...) at most 2 rows name the same one
- adapter_down_factor: bfloat16 [16, 8192, 16], P('row', 'ctx'), may hold values from -0.0625 to 0.0625
- adapter_up_factor: bfloat16 [16, 16, 8192], P('row', None, 'ctx'), may hold values from -1.5 to 1.5
Outputs:
- attended: bfloat16 [64, 8192], P('row', 'ctx')
- mixed: bfloat16 [64, 8192], P('row', 'ctx')
Inputs may be any that keep to these rules, and one draw needn't show every extreme that they name: `row_suffix_length`: some row has exactly 1024 live suffix positions. `row_adapter_index`: among the 4 rows of one index of row (aligned blocks of rows), no adapter is named by more than 2 rows; some adapter is named by exactly 2 rows of a block.
All inputs are finite; a program needn't handle non-finite values.
Results may differ from a plain program's by a relative error of at most 0.006.
Values may be sent and summed in bfloat16 or wider, within the bound.
A program may use at most 64 MiB of HBM per device.

v0:
```python
import math

import jax
import jax.numpy as jnp
from jax import lax
from jax.sharding import PartitionSpec as P

HEADS = 64
KV = 8
HD = 128


def position_blocks(cache):
    count = cache.shape[0]
    width_block = math.gcd(count, 512)
    return cache.reshape(count // width_block, width_block, cache.shape[1], cache.shape[2])


def prefix_maxima(query_heads, keys):
    scale = HD ** (-0.5)
    key_sequence = position_blocks(keys)
    found = []
    for head in range(keys.shape[1]):
        queried = query_heads[:, head]

        def advance(best, key_block):
            scores = (
                jnp.einsum(
                    "rjd,kd->rjk", queried, key_block[:, head], preferred_element_type=jnp.float32
                )
                * scale
            )
            return (jnp.maximum(best, scores.max(-1)), None)

        start = jnp.full(queried.shape[:2], -1e30, jnp.float32)
        best, unused = lax.scan(advance, start, key_sequence)
        found.append(best)
    return jnp.stack(found, axis=1)


def prefix_sums(query_heads, keys, values, ceiling):
    scale = HD ** (-0.5)
    key_sequence = position_blocks(keys)
    value_list = position_blocks(values)
    totals = []
    accums = []
    for head in range(keys.shape[1]):
        queried = query_heads[:, head]
        bound_head = ceiling[:, head]

        def advance(carry, pair):
            total, accum = carry
            key_block, value_block = pair
            scores = (
                jnp.einsum(
                    "rjd,kd->rjk", queried, key_block[:, head], preferred_element_type=jnp.float32
                )
                * scale
            )
            weights = jnp.exp(scores - bound_head[..., None])
            accum = accum + jnp.einsum(
                "rjk,kd->rjd",
                weights.astype(jnp.bfloat16),
                value_block[:, head],
                preferred_element_type=jnp.float32,
            )
            return ((total + weights.sum(-1), accum), None)

        start = (jnp.zeros(queried.shape[:2], jnp.float32), jnp.zeros(queried.shape, jnp.float32))
        (total, accum), unused = lax.scan(advance, start, (key_sequence, value_list))
        totals.append(total)
        accums.append(accum)
    return (jnp.stack(totals, axis=1), jnp.stack(accums, axis=1))


def body(
    queries,
    shared_prefix_cache,
    row_suffix_cache,
    row_suffix_length,
    row_adapter_index,
    adapter_down_factor,
    adapter_up_factor,
):
    own_rows, width = queries.shape
    group = HEADS // KV
    scale = HD ** (-0.5)
    row_index = lax.axis_index("row")
    ctx_index = lax.axis_index("ctx")
    n_ctx = lax.axis_size("ctx")
    n_row = lax.axis_size("row")
    first_row = row_index * own_rows
    rows = own_rows * n_row
    pref_len = shared_prefix_cache.shape[1]
    heads_here = max(1, KV // n_row)
    heads_here = KV
    keys = shared_prefix_cache[0].reshape(pref_len, KV, HD)
    values = shared_prefix_cache[1].reshape(pref_len, KV, HD)
    gathered = lax.all_gather(queries, "row", axis=0, tiled=True)
    query_heads = gathered.reshape(rows, heads_here, group, HD)
    suf_len = row_suffix_cache.shape[2]
    suf_keys = row_suffix_cache[0].reshape(own_rows, suf_len, KV, HD)
    suf_values = row_suffix_cache[1].reshape(own_rows, suf_len, KV, HD)
    own_heads = queries.reshape(own_rows, KV, group, HD)
    positions = ctx_index * suf_len + jnp.arange(suf_len, dtype=jnp.int32)
    valid = (positions[None, :] < row_suffix_length[:, None])[:, None, None, :]
    suf_scores = (
        jnp.einsum("rgjd,rkgd->rgjk", own_heads, suf_keys, preferred_element_type=jnp.float32)
        * scale
    )
    suf_scores = jnp.where(valid, suf_scores, -1e30)
    local = prefix_maxima(query_heads, keys)
    own_part = lax.dynamic_slice_in_dim(local, first_row, own_rows, 0)
    local = lax.dynamic_update_slice_in_dim(
        local, jnp.maximum(own_part, suf_scores.max(-1)), first_row, 0
    )
    top = lax.pmax(local, ("ctx", "row"))
    part_sums, part_outs = prefix_sums(query_heads, keys, values, top)
    feature_width = heads_here * group * HD
    head_width = heads_here * group
    outgoing_out = part_outs.reshape(n_row, own_rows, feature_width)
    outgoing_sum = part_sums.reshape(n_row, own_rows, head_width)
    arrived_out, arrived_sum = (
        lax.all_to_all(outgoing_out, "row", split_axis=0, concat_axis=0, tiled=True),
        lax.all_to_all(outgoing_sum, "row", split_axis=0, concat_axis=0, tiled=True),
    )
    owner_out = arrived_out.sum(0)
    owner_sum = arrived_sum.sum(0)
    own_top = lax.dynamic_slice_in_dim(top, first_row, own_rows, 0)
    suf_weights = jnp.where(valid, jnp.exp(suf_scores - own_top[..., None]), 0.0)
    suf_out = jnp.einsum(
        "rgjk,rkgd->rgjd",
        suf_weights.astype(jnp.bfloat16),
        suf_values,
        preferred_element_type=jnp.float32,
    )
    owner_out = owner_out + suf_out.reshape(own_rows, width)
    owner_sum = owner_sum + suf_weights.sum(-1).reshape(own_rows, HEADS)
    merged_out, merged_sum = (
        lax.psum_scatter(owner_out, "ctx", scatter_dimension=1, tiled=True),
        lax.psum_scatter(owner_sum, "ctx", scatter_dimension=1, tiled=True),
    )
    block_heads = HEADS // n_ctx
    block = width // n_ctx
    attended = (merged_out.reshape(own_rows, block_heads, HD) / merged_sum[..., None]).reshape(
        own_rows, block
    )
    attended = attended.astype(jnp.bfloat16)
    expert_index = row_adapter_index[:, 0]
    resident_experts = adapter_down_factor.shape[0]
    experts_all = resident_experts * n_row
    capacity = max(2, 2 * own_rows // experts_all)
    order = jnp.arange(own_rows, dtype=jnp.int32)
    earlier = (expert_index[:, None] == expert_index[None, :]) & (order[None, :] < order[:, None])
    seat = jnp.sum(earlier.astype(jnp.int32), axis=1)
    slot = expert_index * capacity + seat
    table = (jnp.arange(experts_all * capacity, dtype=jnp.int32)[:, None] == slot[None, :]).astype(
        jnp.bfloat16
    )
    outgoing = jnp.dot(table, attended, preferred_element_type=jnp.float32).astype(jnp.bfloat16)
    outgoing = outgoing.reshape(n_row, resident_experts, capacity, block)
    partial_low = jnp.einsum(
        "sekf,efq->sekq",
        lax.all_to_all(outgoing, "row", split_axis=0, concat_axis=0, tiled=True),
        adapter_down_factor,
        preferred_element_type=jnp.float32,
    )
    low_rank_sum = lax.psum(partial_low, "ctx")
    result = jnp.einsum(
        "mpol,plw->mpow",
        low_rank_sum.astype(jnp.bfloat16),
        adapter_up_factor,
        preferred_element_type=jnp.float32,
    ).astype(jnp.bfloat16)
    returned = lax.all_to_all(result, "row", split_axis=0, concat_axis=0, tiled=True)
    delta = jnp.einsum(
        "so,sf->of",
        table,
        returned.reshape(experts_all * capacity, block),
        preferred_element_type=jnp.float32,
    )
    mixed = (attended.astype(jnp.float32) + delta).astype(jnp.bfloat16)
    return (attended, mixed)


def solution(mesh):
    return jax.shard_map(
        body,
        mesh=mesh,
        in_specs=(
            P("row", None),
            P(None, ("ctx", "row"), None),
            P(None, "row", "ctx", None),
            P("row"),
            P("row", None),
            P("row", "ctx", None),
            P("row", None, "ctx"),
        ),
        out_specs=(P("row", "ctx"), P("row", "ctx")),
        check_vma=False,
    )
```

profile of v0, /device:TPU:1, one launch (start us, length us, event | category | flops | bytes accessed | tf_op | source)
XLA Modules:
  0.0 602.3 jit_solution(17653930991847853728)
XLA Ops:
  7.9 1.8 fusion.66
  11.6 65.5 %all-gather.3.cloned.1.call-done = bf16[16,4,8192]{2,1,0:T(4,128)(2,1)} async-done(((bf16[1,4,8192]{2,1,0:T(4,128)(2,1)}), bf16[16,4,8192]{2,1,0:T(4,128)(2,1)}) %all-gather.3.cloned.1.call-update) | async-done | bytes 1048592 | tf_op jit(solution)/shard_map/all_gather | solution.py:99
  77.0 2.1 reshape.166
  82.9 1.9 fusion.68
  84.8 1.9 fusion.67
  92.8 1.4 fusion.55
  94.2 111.3 %pmax.7 = f32[64,8,8]{2,0,1:T(8,128)S(1)} all-reduce(f32[64,8,8]{2,0,1:T(8,128)} %fusion.55), channel_id=1, replica_groups=mesh['ctx'=32,'row'=16] {'ctx','row'}, use_global_device_ids=true, to_apply=%region_9.10 | all-reduce | flops 4096 | bytes 32768 | tf_op jit(solution)/shard_map/pmax | solution.py:117
  205.6 1.6 fusion.11
  209.4 1.7 reshape.170
  211.0 1.4 reshape.204
  212.5 6.8 %all-to-all-start.1 = ((f32[16,1,256]{2,1,0:T(1,128)}), f32[16,1,256]{2,1,0:T(1,128)}, u32[]{:S(2)}, u32[]{:S(2)}) async-start(f32[16,1,256]{2,1,0:T(1,128)} %reshape.204), calls=%async_computation.1 | async-start | bytes 32768 | tf_op jit(solution)/shard_map/all_to_all | solution.py:125
  219.3 1.4 fusion.7
  220.7 1.3 fusion.6
  225.0 1.9 reshape.168
  226.9 3.9 all-to-all-done.1
  230.8 7.7 %all-to-all-start = ((f32[16,4,8192]{2,1,0:T(4,128)}), f32[16,4,8192]{2,1,0:T(4,128)S(1)}, u32[]{:S(2)}, u32[]{:S(2)}) async-start(f32[16,4,8192]{2,1,0:T(4,128)} %reshape.168), calls=%async_computation | async-start | bytes 4194304 | tf_op jit(solution)/shard_map/all_to_all | solution.py:124
  241.8 1.4 reduce
  243.3 65.6 %all-reduce = f32[4,64]{1,0:T(4,128)S(1)} all-reduce(f32[4,64]{1,0:T(4,128)S(1)} %add.105), channel_id=3, replica_groups=mesh['ctx'=32,'row'=16] {'ctx'}, use_global_device_ids=true, to_apply=%region_22.23.clone | all-reduce | flops 256 | bytes 2048
  309.0 21.3 %all-to-all-done = f32[16,4,8192]{2,1,0:T(4,128)S(1)} async-done(((f32[16,4,8192]{2,1,0:T(4,128)}), f32[16,4,8192]{2,1,0:T(4,128)S(1)}, u32[]{:S(2)}, u32[]{:S(2)}) %all-to-all-start) | async-done | bytes 2097184 | tf_op jit(solution)/shard_map/all_to_all | solution.py:124
  330.8 2.6 copy.182
  333.5 101.0 %reduce-scatter.5.cloned.1.call-done = f32[256,4]{1,0:T(8,128)} async-done(((f32[8192,4]{1,0:T(8,128)}), f32[256,4]{1,0:T(8,128)}) %reduce-scatter.5.cloned.1.call-update) | async-done | bytes 4112
  435.7 23.2 %all_to_all.20 = bf16[16,1,2,256]{3,2,1,0:T(2,128)(2,1)S(1)} all-to-all(bf16[16,1,2,256]{3,2,1,0:T(2,128)(2,1)S(1)} %bitcast.325), channel_id=1, replica_groups=mesh['ctx'=32,'row'=16] {'row'}, dimensions={0} | all-to-all | bytes 32768 | tf_op jit(solution)/shard_map/all_to_all | solution.py:164
  459.0 121.7 %psum.7 = bf16[16,1,2,16]{3,0,2,1:T(8,128)(2,1)S(1)} all-reduce(f32[16,1,2,16]{3,0,2,1:T(8,128)S(1)} %convolution_bitcast_fusion.9), channel_id=1, replica_groups=mesh['ctx'=32,'row'=16] {'ctx'}, use_global_device_ids=true, to_apply=%region_24.25 | all-reduce | flops 512 | bytes 3072 | tf_op jit(solution)/shard_map/psum | solution.py:168
  580.8 13.8 %all_to_all.21 = bf16[16,1,2,256]{3,2,1,0:T(2,128)(2,1)S(1)} all-to-all(bf16[16,1,2,256]{3,2,1,0:T(2,128)(2,1)S(1)} %copy.181), channel_id=1, replica_groups=mesh['ctx'=32,'row'=16] {'row'}, dimensions={0} | all-to-all | bytes 32768 | tf_op jit(solution)/shard_map/all_to_all | solution.py:175
  (119 shorter events, 22.6 us)
Async XLA Ops:
  7.2 573.5 %copy-start = (bf16[1,16,256]{2,1,0:T(8,128)(2,1)S(1)}, bf16[1,16,256]{2,1,0:T(8,128)(2,1)}, u32[]{:S(2)}) copy-start(bf16[1,16,256]{2,1,0:T(8,128)(2,1)} %param.13) | copy-start | bytes 24580
  7.2 2.6 copy-start.4
  7.2 69.8 %all-gather.3.cloned.1.call-start = ((), (), s32[]{:S(2)}) async-start(), calls=%async_computation.5 | async-start | bytes 1114112 | tf_op jit(solution)/shard_map/all_gather | solution.py:99
  11.1 69.3 %copy-start.3 = (bf16[1,256,1024]{1,2,0:T(8,128)(2,1)}, bf16[1,256,1024]{1,2,0:T(8,128)(2,1)S(1)}, u32[]{:S(2)}) copy-start(bf16[1,256,1024]{1,2,0:T(8,128)(2,1)S(1)} %copy.186) | copy-start | bytes 1572868
  205.5 1.7 copy-start.17
  205.6 2.8 copy-start.6
  205.6 2.8 copy-start.8
  205.6 2.8 copy-start.10
  205.6 2.8 copy-start.12
  205.6 2.8 copy-start.14
  205.6 2.8 copy-start.16
  212.5 18.3 %all-to-all-start.1 = ((f32[16,1,256]{2,1,0:T(1,128)}), f32[16,1,256]{2,1,0:T(1,128)}, u32[]{:S(2)}, u32[]{:S(2)}) async-start(f32[16,1,256]{2,1,0:T(1,128)} %reshape.204), calls=%async_computation.1 | async-start | bytes 32768 | tf_op jit(solution)/shard_map/all_to_all | solution.py:125
  219.3 3.9 copy-start.2
  219.3 3.9 copy-start.15
  219.3 4.2 copy-start.13
  219.3 4.5 copy-start.11
  220.7 3.4 copy-start.9
  222.1 2.3 copy-start.7
  226.9 11.6 %copy-start.5 = (bf16[1,4,32,1024]{3,2,1,0:T(8,128)(2,1)S(1)}, bf16[1,4,32,1024]{3,2,1,0:T(8,128)(2,1)}, u32[]{:S(2)}) copy-start(bf16[1,4,32,1024]{3,2,1,0:T(8,128)(2,1)} %get-tuple-element.184) | copy-start | bytes 786436
  226.9 13.6 %copy-start.23 = (s32[4,1]{0,1:T(1,128)S(1)}, s32[4,1]{0,1:T(1,128)}, u32[]{:S(2)}) copy-start(s32[4,1]{0,1:T(1,128)} %param.11) | copy-start | bytes 52
  230.8 99.5 %all-to-all-start = ((f32[16,4,8192]{2,1,0:T(4,128)}), f32[16,4,8192]{2,1,0:T(4,128)S(1)}, u32[]{:S(2)}, u32[]{:S(2)}) async-start(f32[16,4,8192]{2,1,0:T(4,128)} %reshape.168), calls=%async_computation | async-start | bytes 4194304 | tf_op jit(solution)/shard_map/all_to_all | solution.py:124
  238.4 196.1 %reduce-scatter.5.cloned.1.call-start = ((), (), s32[]{:S(2)}) async-start(), calls=%async_computation.6 | async-start | bytes 4325376
  333.4 125.5 %copy-start.20 = (bf16[1,256,16]{1,2,0:T(8,128)(2,1)S(1)}, bf16[1,256,16]{1,2,0:T(8,128)(2,1)}, u32[]{:S(2)}) copy-start(bf16[1,256,16]{1,2,0:T(8,128)(2,1)} %param.12) | copy-start | bytes 24580
  435.5 159.9 %copy-start.21 = (bf16[4,256]{1,0:T(4,128)(2,1)}, bf16[4,256]{1,0:T(4,128)(2,1)S(1)}, u32[]{:S(2)}) copy-start(bf16[4,256]{1,0:T(4,128)(2,1)S(1)} %fusion.62) | copy-start | bytes 6148
  (4 other events, 5.5 us)
Sparse Core Ops, SparseCore 0:
  10.1 66.8 all-gather.2
  333.5 100.9 reduce-scatter.4
where the time goes:
time: 607 us; the launch traced here: 602 us
  blocking collectives  336 us (55%)
  waiting for transfers between devices  192 us (32%)
  local copies, waits for them, and re-layouts  17.8 us (3%)
  between operations  15.4 us (3%)
  matrix products  15.3 us (3%)
  starting transfers between devices  14.5 us (2%)
  other arithmetic  11.3 us (2%)
    psum x1, blocking collectives, body(): low_rank_sum = lax.psum(partial_low, 'ctx')  122 us
    pmax x1, blocking collectives, body(): top = lax.pmax(local, ('ctx', 'row'))  111 us
    unnamed x3, waiting for transfers between devices  102 us
    unnamed x1, blocking collectives  65.6 us
    all_gather x1, waiting for transfers between devices, body(): gathered = lax.all_gather(queries, 'row', axis=0, tiled=True)  65.5 us
    all_to_all x1, blocking collectives, body(): lax.all_to_all(outgoing, 'row', split_axis=0, concat_axis=0, tiled=True)  23.2 us
    all_to_all x1, waiting for transfers between devices, body(): lax.all_to_all(outgoing_out, 'row', split_axis=0, concat_axis=0, tiled=True)  21.3 us
    all_to_all x1, blocking collectives, body(): lax.all_to_all(result, 'row', split_axis=0, concat_axis=0, tiled=True)  13.8 us
  transfers between devices with their start and end apart: 4, of which 4 were waited for; matrix products, arithmetic and copies ran while one was open for 3% of the time, Pallas kernels for 0%

commit v1 on v0

v1 whole, which is shorter than its diff:
```python
import functools
import math

import jax
import jax.numpy as jnp
from jax import lax
from jax.experimental import pallas as pl
from jax.experimental.pallas import tpu as pltpu
from jax.sharding import PartitionSpec as P

HD = 128
GROUP = 8
OWN = 4
VEC = 16
EXTRA = 16
MESH = pl.DeviceIdType.MESH
F32 = jnp.float32
BF16 = jnp.bfloat16


def three(value):
    high = value.astype(BF16).astype(F32)
    rest = value - high
    middle = rest.astype(BF16).astype(F32)
    return [high, middle, rest - middle]


def stacked(rows, count):
    width = rows[0].shape[1]
    at = lax.broadcasted_iota(jnp.int32, (count, width), 0)
    out = jnp.zeros((count, width), F32)
    for index, row in enumerate(rows):
        out = jnp.where(at == index, jnp.broadcast_to(row, (count, width)), out)
    return out


def contract_last(a, b):
    return lax.dot_general(a, b, (((1,), (1,)), ((), ())), preferred_element_type=F32)


def kernel(
    n_ctx,
    n_row,
    q_hbm,
    kv_hbm,
    suf_hbm,
    len_ref,
    idx_ref,
    down_hbm,
    up_hbm,
    att_ref,
    mix_ref,
    qv,
    q32,
    qown,
    kvs,
    vt,
    bias,
    qbuf,
    obuf,
    rbuf,
    zs,
    zr,
    ad,
    ls,
    lr,
    s_q,
    s_loc,
    s_sib_send,
    s_sib_recv,
    s_ad_loc,
    s_ad_send,
    s_ad_recv,
    s_a1_send,
    s_a1_recv,
    s_a2_send,
    s_a2_recv,
    s_o_send,
    s_o_recv,
    s_z_send,
    s_z_recv,
    s_l_send,
    s_l_recv,
):
    chips = n_ctx // 2
    pairs = chips // 2
    half = n_row // 2
    lanes = half * VEC
    pd = kv_hbm.shape[1]
    sd = suf_hbm.shape[1]
    spos = sd // OWN
    scale = HD**-0.5 * math.log2(math.e)

    ctx = lax.axis_index("ctx")
    z = lax.axis_index("row")
    c = lax.rem(ctx, 2)
    chip = ctx // 2
    g0 = chip // 2
    yl = lax.rem(chip, 2)
    zi = z // 2
    zp = lax.rem(z, 2)
    ablk = lax.rem(z + yl, 2)
    blk = g0 * 2 + ablk
    sib = ctx + 1 - 2 * c
    mate = ctx + 2 - 4 * yl

    q_copy = pltpu.make_async_copy(q_hbm, qv, s_q)
    q_copy.start()
    loc = []
    for i in range(2):
        loc.append(pltpu.make_async_copy(kv_hbm.at[i], kvs.at[i, 0:pd], s_loc.at[2 * i]))
        loc.append(
            pltpu.make_async_copy(
                suf_hbm.at[i], kvs.at[i, 2 * pd : 2 * pd + sd], s_loc.at[2 * i + 1]
            )
        )
    for copy in loc:
        copy.start()
    ad_loc = [
        pltpu.make_async_copy(down_hbm.at[0], ad.at[z, 0], s_ad_loc.at[0]),
        pltpu.make_async_copy(up_hbm.at[0], ad.at[z, 1], s_ad_loc.at[1]),
    ]
    for copy in ad_loc:
        copy.start()

    barrier = pltpu.get_barrier_semaphore()

    def greet_plane(d, carry):
        pl.semaphore_signal(
            barrier, 1, device_id=(lax.rem(ctx + d, n_ctx), z), device_id_type=MESH
        )
        return carry

    def greet_line(d, carry):
        pl.semaphore_signal(
            barrier, 1, device_id=(ctx, lax.rem(z + d, n_row)), device_id_type=MESH
        )
        return carry

    def greet_mate(i, carry):
        pl.semaphore_signal(
            barrier,
            1,
            device_id=(mate, lax.rem(z + 2 * i + 1 - yl, n_row)),
            device_id_type=MESH,
        )
        return carry

    lax.fori_loop(1, n_ctx, greet_plane, 0)
    lax.fori_loop(1, n_row, greet_line, 0)
    lax.fori_loop(yl, half, greet_mate, 0)

    q_copy.wait()
    for hh in range(4):
        head = g0 * GROUP + 4 * (hh // 2) + 2 * c + hh % 2
        start = pl.multiple_of(head * HD, HD)
        q32[hh * OWN : (hh + 1) * OWN, :] = qv[:, pl.ds(start, HD)].astype(F32)
    qown[...] = q32[...].astype(BF16)

    pl.semaphore_wait(barrier, n_ctx - 1 + n_row - 1 + half - 1 + yl)

    slot = g0 * 2 + zp
    place = pl.ds(pl.multiple_of(zi * VEC, VEC), VEC)

    def send_a1(i, carry):
        target = 2 * lax.rem(zi + i, half) + ablk
        pltpu.make_async_remote_copy(
            src_ref=qown,
            dst_ref=qbuf.at[slot, place],
            send_sem=s_a1_send,
            recv_sem=s_a1_recv,
            device_id=(ctx, target),
            device_id_type=MESH,
        ).start()
        return carry

    lax.fori_loop(1 - yl, half, send_a1, 0)

    @pl.when(yl == 0)
    def _():
        pltpu.make_async_copy(qown, qbuf.at[slot, place], s_a1_recv).start()

    sibling = []
    for i in range(2):
        sibling.append(
            pltpu.make_async_remote_copy(
                src_ref=kv_hbm.at[i],
                dst_ref=kvs.at[i, pd : 2 * pd],
                send_sem=s_sib_send.at[2 * i],
                recv_sem=s_sib_recv.at[2 * i],
                device_id=(sib, z),
                device_id_type=MESH,
            )
        )
        sibling.append(
            pltpu.make_async_remote_copy(
                src_ref=suf_hbm.at[i],
                dst_ref=kvs.at[i, 2 * pd + sd : 2 * pd + 2 * sd],
                send_sem=s_sib_send.at[2 * i + 1],
                recv_sem=s_sib_recv.at[2 * i + 1],
                device_id=(sib, z),
                device_id_type=MESH,
            )
        )
    for copy in sibling:
        copy.start()

    at = lax.broadcasted_iota(jnp.int32, (2 * sd, lanes), 0)
    lane = lax.broadcasted_iota(jnp.int32, (2 * sd, lanes), 1)
    owner = lax.rem(at, sd) // spos
    holder = jnp.where(at < sd, ctx, sib)
    position = holder * spos + lax.rem(at, spos)
    live = jnp.zeros((2 * sd, lanes), jnp.int32)
    for k in range(OWN):
        live = jnp.where(owner == k, len_ref[k], live)
    valid = (lane // VEC == zi) & (lax.rem(lane, OWN) == owner) & (position < live)
    bias[...] = jnp.where(valid, 0.0, -1e30).astype(F32)

    pltpu.make_async_copy(qbuf.at[blk], qbuf.at[blk], s_a1_recv).wait()

    def send_a2(i, carry):
        target = lax.rem(g0 + pairs - i // 2, pairs) * 2 + lax.rem(yl + i, 2)
        pltpu.make_async_remote_copy(
            src_ref=qbuf.at[blk],
            dst_ref=qbuf.at[blk],
            send_sem=s_a2_send,
            recv_sem=s_a2_recv.at[blk],
            device_id=(target * 2 + c, z),
            device_id_type=MESH,
        ).start()
        return carry

    lax.fori_loop(1, chips, send_a2, 0)

    for copy in ad_loc:
        copy.wait()

    def send_ad(d, carry):
        pltpu.make_async_remote_copy(
            src_ref=ad.at[z],
            dst_ref=ad.at[z],
            send_sem=s_ad_send,
            recv_sem=s_ad_recv,
            device_id=(ctx, lax.rem(z + d, n_row)),
            device_id_type=MESH,
        ).start()
        return carry

    lax.fori_loop(1, n_row, send_ad, 0)

    for copy in loc:
        copy.wait()
    for copy in sibling:
        copy.wait()

    def turn_values(g, carry):
        columns = pl.ds(pl.multiple_of(g * HD, HD), HD)
        vt[g] = kvs[1, :, columns].T
        return carry

    lax.fori_loop(0, pairs, turn_values, 0)

    def attend(t, carry):
        g = lax.rem(g0 + t, pairs)
        for a in range(2):

            @pl.when(2 * g + a != blk)
            def _():
                pltpu.make_async_copy(
                    qbuf.at[2 * g + a], qbuf.at[2 * g + a], s_a2_recv.at[2 * g + a]
                ).wait()

        columns = pl.ds(pl.multiple_of(g * HD, HD), HD)
        sides = (zp, 1 - zp)
        near = qbuf[2 * g + zp]
        both = jnp.concatenate([near, qbuf[2 * g + 1 - zp]], axis=0)
        scores = contract_last(kvs[0, 0 : 2 * pd, columns], both) * scale
        suffix = contract_last(kvs[0, 2 * pd : 2 * pd + 2 * sd, columns], near) * scale
        suffix = suffix + bias[...]
        top = jnp.max(scores, axis=0, keepdims=True)
        top_near = jnp.maximum(top[:, :lanes], jnp.max(suffix, axis=0, keepdims=True))
        top = jnp.concatenate([top_near, top[:, lanes:]], axis=1)
        weights = jnp.exp2(scores - top)
        weights_near = jnp.exp2(suffix - top_near)
        total = jnp.sum(weights, axis=0, keepdims=True)
        total_near = jnp.sum(weights_near, axis=0, keepdims=True)
        acc = jnp.dot(
            vt[g, :, 0 : 2 * pd], weights.astype(BF16), preferred_element_type=F32
        )
        acc_near = jnp.dot(
            vt[g, :, 2 * pd : 2 * pd + 2 * sd],
            weights_near.astype(BF16),
            preferred_element_type=F32,
        )
        outs = (acc[:, :lanes] + acc_near, acc[:, lanes:])
        tops = (top_near, top[:, lanes:])
        totals = (total[:, :lanes] + total_near, total[:, lanes:])
        for j in range(2):
            index = 2 * g + sides[j]
            obuf[index, 0:HD, :] = outs[j].astype(BF16)
            obuf[index, HD : HD + EXTRA, :] = stacked(
                three(tops[j]) + three(totals[j]), EXTRA
            ).astype(BF16)
            target = 2 * g + lax.rem(sides[j] + z, 2)

            @pl.when(target != chip)
            def _():
                pltpu.make_async_remote_copy(
                    src_ref=obuf.at[index],
                    dst_ref=rbuf.at[chip],
                    send_sem=s_o_send,
                    recv_sem=s_o_recv,
                    device_id=(target * 2 + c, z),
                    device_id_type=MESH,
                ).start()

            @pl.when(target == chip)
            def _():
                pltpu.make_async_copy(obuf.at[index], rbuf.at[chip], s_o_recv).start()

        return carry

    lax.fori_loop(0, pairs, attend, 0)

    pltpu.make_async_copy(rbuf, rbuf, s_o_recv).wait()
    tops, totals = [], []
    for k in range(chips):
        extra = rbuf[k, HD : HD + EXTRA, :].astype(F32)
        tops.append(extra[0:1] + extra[1:2] + extra[2:3])
        totals.append(extra[3:4] + extra[4:5] + extra[5:6])
    top = functools.reduce(jnp.maximum, tops)
    acc = jnp.zeros((HD, lanes), F32)
    total = jnp.zeros((1, lanes), F32)
    for k in range(chips):
        factor = jnp.exp2(tops[k] - top)
        acc = acc + factor * rbuf[k, 0:HD, :].astype(F32)
        total = total + factor * totals[k]
    extra = stacked(three(top) + three(total), HD)
    zs[...] = jnp.concatenate(
        [acc.T.reshape(half, 2, 8, HD), extra.T.reshape(half, 2, 8, HD)], axis=2
    ).astype(BF16)

    def send_z(i, carry):
        at_z = lax.rem(zi + i, half)
        target_z = 2 * at_z + ablk
        for side in range(2):
            target = (g0 * 2 + side) * 2 + c
            here = (target == ctx) & (target_z == z)

            @pl.when(jnp.logical_not(here))
            def _():
                pltpu.make_async_remote_copy(
                    src_ref=zs.at[at_z, side],
                    dst_ref=zr.at[z],
                    send_sem=s_z_send,
                    recv_sem=s_z_recv,
                    device_id=(target, target_z),
                    device_id_type=MESH,
                ).start()

            @pl.when(here)
            def _():
                pltpu.make_async_copy(zs.at[at_z, side], zr.at[z], s_z_recv).start()

        return carry

    lax.fori_loop(0, half, send_z, 0)

    pltpu.make_async_copy(ad.at[0 : n_row - 1], ad.at[0 : n_row - 1], s_ad_recv).wait()

    pltpu.make_async_copy(zr, zr, s_z_recv).wait()
    arrived = zr[...].astype(F32)
    extra = arrived[:, 8:16, :].reshape(n_row * 8, HD).astype(BF16)
    row = lax.broadcasted_iota(jnp.int32, (HD, 2 * HD), 0)
    col = lax.broadcasted_iota(jnp.int32, (HD, 2 * HD), 1)
    pick = jnp.where(row // 3 == col // HD, 1.0, 0.0).astype(BF16)
    spread = jnp.dot(extra, pick, preferred_element_type=F32)
    tops = spread[:, :HD].reshape(n_row, 8, HD)
    totals = spread[:, HD:].reshape(n_row, 8, HD)
    factor = jnp.exp2(tops - jnp.max(tops, axis=0, keepdims=True))
    acc = jnp.sum(factor * arrived[:, 0:8, :], axis=0)
    total = jnp.sum(factor * totals, axis=0)
    attended = (acc / total).astype(BF16).astype(F32)
    attended = jnp.concatenate([attended[0:OWN], attended[OWN : 2 * OWN]], axis=1)
    att_ref[...] = attended.astype(BF16)

    rank = down_hbm.shape[1]
    width = n_row * rank // 2
    twice = jnp.concatenate([attended, attended], axis=0).astype(BF16)
    low = contract_last(twice, ad[:, 0].reshape(n_row * rank, 2 * HD))
    row = lax.broadcasted_iota(jnp.int32, (2 * OWN, width), 0)
    col = lax.broadcasted_iota(jnp.int32, (2 * OWN, width), 1)
    wanted = jnp.zeros((2 * OWN, width), jnp.int32)
    for k in range(OWN):
        wanted = jnp.where(lax.rem(row, OWN) == k, idx_ref[k, 0], wanted)
    mine = wanted == col // rank + (n_row // 2) * (row // OWN)
    low = jnp.where(row < OWN, low[:, :width], low[:, width:])
    ls[...] = jnp.where(mine, low, 0.0)
    lr[ctx] = ls[...]

    def send_l(d, carry):
        pltpu.make_async_remote_copy(
            src_ref=ls,
            dst_ref=lr.at[ctx],
            send_sem=s_l_send,
            recv_sem=s_l_recv,
            device_id=(lax.rem(ctx + d, n_ctx), z),
            device_id_type=MESH,
        ).start()
        return carry

    lax.fori_loop(1, n_ctx, send_l, 0)
    pltpu.make_async_copy(lr.at[0 : n_ctx - 1], lr.at[0 : n_ctx - 1], s_l_recv).wait()
    low = jnp.sum(lr[...], axis=0).astype(BF16)
    up = ad[:, 1].reshape(n_row * rank, 2 * HD)
    first = jnp.dot(low, up[:width], preferred_element_type=F32)
    second = jnp.dot(low, up[width:], preferred_element_type=F32)
    delta = first[0:OWN] + second[OWN : 2 * OWN]
    mix_ref[...] = (attended + delta.astype(BF16).astype(F32)).astype(BF16)

    @pl.when(yl == 0)
    def _():
        part = qbuf.at[0, 0 : lanes - VEC]
        pltpu.make_async_copy(part, part, s_a1_send).wait()
        part = zr.at[0 : n_row - 1]
        pltpu.make_async_copy(part, part, s_z_send).wait()

    @pl.when(yl == 1)
    def _():
        pltpu.make_async_copy(qbuf.at[0], qbuf.at[0], s_a1_send).wait()
        pltpu.make_async_copy(zr, zr, s_z_send).wait()

    part = qbuf.at[0 : chips - 1]
    pltpu.make_async_copy(part, part, s_a2_send).wait()
    part = obuf.at[0 : chips - 1]
    pltpu.make_async_copy(part, part, s_o_send).wait()
    part = ad.at[0 : n_row - 1]
    pltpu.make_async_copy(part, part, s_ad_send).wait()
    part = lr.at[0 : n_ctx - 1]
    pltpu.make_async_copy(part, part, s_l_send).wait()


def body(n_ctx, n_row, queries, prefix, suffix, lengths, adapters, down, up):
    chips = n_ctx // 2
    pairs = chips // 2
    half = n_row // 2
    lanes = half * VEC
    pd = prefix.shape[1]
    sd = suffix.shape[1] * suffix.shape[2]
    width = prefix.shape[2]
    rank = down.shape[2]
    suffix = suffix.reshape(2, sd, width)
    down = jnp.transpose(down, (0, 2, 1))
    hbm = pl.BlockSpec(memory_space=pl.ANY)
    smem = pl.BlockSpec(memory_space=pltpu.SMEM)
    vmem = pl.BlockSpec(memory_space=pltpu.VMEM)
    dma = pltpu.SemaphoreType.DMA
    out = jax.ShapeDtypeStruct((OWN, 2 * HD), BF16)
    return pl.pallas_call(
        functools.partial(kernel, n_ctx, n_row),
        out_shape=(out, out),
        in_specs=[hbm, hbm, hbm, smem, smem, hbm, hbm],
        out_specs=(vmem, vmem),
        scratch_shapes=[
            pltpu.VMEM(queries.shape, BF16),
            pltpu.VMEM((VEC, HD), F32),
            pltpu.VMEM((VEC, HD), BF16),
            pltpu.VMEM((2, 2 * pd + 2 * sd, width), BF16),
            pltpu.VMEM((pairs, HD, 2 * pd + 2 * sd), BF16),
            pltpu.VMEM((2 * sd, lanes), F32),
            pltpu.VMEM((chips, lanes, HD), BF16),
            pltpu.VMEM((chips, HD + EXTRA, lanes), BF16),
            pltpu.VMEM((chips, HD + EXTRA, lanes), BF16),
            pltpu.VMEM((half, 2, 16, HD), BF16),
            pltpu.VMEM((n_row, 16, HD), BF16),
            pltpu.VMEM((n_row, 2, rank, 2 * HD), BF16),
            pltpu.VMEM((2 * OWN, n_row * rank // 2), F32),
            pltpu.VMEM((n_ctx, 2 * OWN, n_row * rank // 2), F32),
            dma,
            dma((4,)),
            dma((4,)),
            dma((4,)),
            dma((2,)),
            dma,
            dma,
            dma,
            dma,
            dma,
            dma((chips,)),
            dma,
            dma,
            dma,
            dma,
            dma,
            dma,
        ],
        compiler_params=pltpu.CompilerParams(
            collective_id=0, has_side_effects=True, vmem_limit_bytes=40 * 1024 * 1024
        ),
        name="decode_attention",
    )(queries, prefix, suffix, lengths, adapters, down, up)


def solution(mesh):
    return jax.shard_map(
        functools.partial(body, mesh.shape["ctx"], mesh.shape["row"]),
        mesh=mesh,
        in_specs=(
            P("row", None),
            P(None, ("ctx", "row"), None),
            P(None, "row", "ctx", None),
            P("row"),
            P("row", None),
            P("row", "ctx", None),
            P("row", None, "ctx"),
        ),
        out_specs=(P("row", "ctx"), P("row", "ctx")),
        check_vma=False,
    )
```

time: 607 us -> 68.1 us (0.11)
  blocking collectives: 336 us -> 0 us
  waiting for transfers between devices: 192 us -> 0 us
  Pallas kernels: 0 us -> 60.1 us
  matrix products: 15.3 us -> 0 us
  between operations: 15.4 us -> 0.65 us
  starting transfers between devices: 14.5 us -> 0 us
  other arithmetic: 11.3 us -> 0 us
  local copies, waits for them, and re-layouts: 17.8 us -> 6.96 us
    psum x1 -> x0, blocking collectives: 122 us -> none  [body(): low_rank_sum = lax.psum(partial_low, 'ctx')]
    pmax x1 -> x0, blocking collectives: 111 us -> none  [body(): top = lax.pmax(local, ('ctx', 'row'))]
    unnamed x3 -> x0, waiting for transfers between devices: 102 us -> none
    unnamed x1 -> x0, blocking collectives: 65.6 us -> none
    all_gather x1 -> x0, waiting for transfers between devices: 65.5 us -> none  [body(): gathered = lax.all_gather(queries, 'row', axis=0, tiled=True)]
    pallas_call x0 -> x1, Pallas kernels: none -> 60.1 us  [body(): pl.pallas_call(functools.partial(kernel, n_ctx, n_row), out_shape=(out, o...]
    all_to_all x2 -> x0, blocking collectives: 37 us -> none  [the longest x1 23.2 us: body(): lax.all_to_all(outgoing, 'row', split_axis=0, concat_axis=0, tiled=True)]
    all_to_all x2 -> x0, waiting for transfers between devices: 25.2 us -> none  [the longest x1 21.3 us: body(): lax.all_to_all(outgoing_out, 'row', split_axis=0, concat_axis=0, tiled=True)]
  transfers between devices with their start and end apart: 4 -> 0, of which waited for: 4 -> 0; matrix products, arithmetic and copies ran while one was open for 3% -> 0% of each run, Pallas kernels for 0% -> 0%
where the time goes in v1:
time: 68.1 us; the launch traced here: 67.7 us
  Pallas kernels  60.1 us (88%)
  local copies, waits for them, and re-layouts  6.96 us (10%)
    pallas_call x1, Pallas kernels, body(): pl.pallas_call(functools.partial(kernel, n_ctx, n_row), out_shape=(out, o...  60.1 us
    unnamed x17, local copies, waits for them, and re-layouts  6.96 us

profile of v1, /device:TPU:1, one launch (start us, length us, event | category | flops | bytes accessed | tf_op | source)
XLA Modules:
  0.0 67.7 jit_solution(2381006533262790929)
XLA Ops:
  0.6 0.0 copy-start.6
  0.6 0.6 copy-done.6
  1.3 0.0 copy-start.5
  1.3 0.1 copy.9.idx_ref
  1.4 0.6 copy-done.5
  1.9 0.0 copy-start
  1.9 1.2 %copy-done = bf16[2,256,1024]{2,1,0:T(8,128)(2,1)S(1)} copy-done((bf16[2,256,1024]{2,1,0:T(8,128)(2,1)S(1)}, bf16[2,256,1024]{2,1,0:T(8,128)(2,1)}, u32[]{:S(2)}) %copy-start) | copy-done | bytes 1048600
  3.2 0.0 copy-start.1
  3.2 1.0 %copy-done.1 = bf16[2,4,32,1024]{3,2,1,0:T(8,128)(2,1)S(1)} copy-done((bf16[2,4,32,1024]{3,2,1,0:T(8,128)(2,1)S(1)}, bf16[2,4,32,1024]{3,2,1,0:T(8,128)(2,1)}, u32[]{:S(2)}) %copy-start.1) | copy-done | bytes 524312
  4.2 0.0 copy-start.2
  4.2 0.8 %copy-done.2 = bf16[4,8192]{1,0:T(4,128)(2,1)S(1)} copy-done((bf16[4,8192]{1,0:T(4,128)(2,1)S(1)}, bf16[4,8192]{1,0:T(4,128)(2,1)}, u32[]{:S(2)}) %copy-start.2) | copy-done | bytes 65560
  5.0 0.0 copy-start.3
  5.1 0.7 %copy-done.3 = bf16[1,256,16]{1,2,0:T(8,128)(2,1)S(1)} copy-done((bf16[1,256,16]{1,2,0:T(8,128)(2,1)S(1)}, bf16[1,256,16]{1,2,0:T(8,128)(2,1)}, u32[]{:S(2)}) %copy-start.3) | copy-done | bytes 8216
  5.7 0.0 copy-start.4
  5.7 0.7 %copy-done.4 = bf16[1,16,256]{2,1,0:T(8,128)(2,1)S(1)} copy-done((bf16[1,16,256]{2,1,0:T(8,128)(2,1)S(1)}, bf16[1,16,256]{2,1,0:T(8,128)(2,1)}, u32[]{:S(2)}) %copy-start.4) | copy-done | bytes 8216
  6.4 60.1 %decode_attention.1 = (bf16[4,256]{1,0:T(4,128)(2,1)S(1)}, bf16[4,256]{1,0:T(4,128)(2,1)S(1)}) custom-call(bf16[4,8192]{1,0:T(4,128)(2,1)S(1)} %copy-done.2, bf16[2,256,1024]{2,1,0:T(8,128)(2,1)S(1)} %copy-done, bf16[2,128,1024]{2,1,0:T(8,128)(2,1)S(1)} %bitcast.2, s32[4]{0:T(128)S(1)} %copy-done.5, s32[4,1]{1,0:T(4,128)S(1)} %copy.9.idx_ref, ...), custom_call_target="tpu_custom_call" | custom-call | tf_op jit(solution)/shard_map/decode_attention/pallas_call | solution.py:459
  66.6 0.6 copy.12
  67.2 0.6 copy.13
Async XLA Ops:
  0.6 0.7 copy-start.6
  1.3 0.7 copy-start.5
  1.9 1.2 %copy-start = (bf16[2,256,1024]{2,1,0:T(8,128)(2,1)S(1)}, bf16[2,256,1024]{2,1,0:T(8,128)(2,1)}, u32[]{:S(2)}) copy-start(bf16[2,256,1024]{2,1,0:T(8,128)(2,1)} %kv_hbm.1) | copy-start | bytes 3145732
  3.2 1.0 %copy-start.1 = (bf16[2,4,32,1024]{3,2,1,0:T(8,128)(2,1)S(1)}, bf16[2,4,32,1024]{3,2,1,0:T(8,128)(2,1)}, u32[]{:S(2)}) copy-start(bf16[2,4,32,1024]{3,2,1,0:T(8,128)(2,1)} %param.9) | copy-start | bytes 1572868
  4.2 0.8 %copy-start.2 = (bf16[4,8192]{1,0:T(4,128)(2,1)S(1)}, bf16[4,8192]{1,0:T(4,128)(2,1)}, u32[]{:S(2)}) copy-start(bf16[4,8192]{1,0:T(4,128)(2,1)} %q_hbm.1) | copy-start | bytes 196612
  5.0 0.7 %copy-start.3 = (bf16[1,256,16]{1,2,0:T(8,128)(2,1)S(1)}, bf16[1,256,16]{1,2,0:T(8,128)(2,1)}, u32[]{:S(2)}) copy-start(bf16[1,256,16]{1,2,0:T(8,128)(2,1)} %param.12) | copy-start | bytes 24580
  5.7 0.7 %copy-start.4 = (bf16[1,16,256]{2,1,0:T(8,128)(2,1)S(1)}, bf16[1,16,256]{2,1,0:T(8,128)(2,1)}, u32[]{:S(2)}) copy-start(bf16[1,16,256]{2,1,0:T(8,128)(2,1)} %up_hbm.1) | copy-start | bytes 24580

commit v2 on v1

v2 whole, which is shorter than its diff:
```python
import functools
import math

import jax
import jax.numpy as jnp
from jax import lax
from jax.experimental import pallas as pl
from jax.experimental.pallas import tpu as pltpu
from jax.sharding import PartitionSpec as P

HD = 128
GROUP = 8
OWN = 4
VEC = 16
EXTRA = 16
COLUMN = 4
MESH = pl.DeviceIdType.MESH
F32 = jnp.float32
BF16 = jnp.bfloat16


def three(value):
    high = value.astype(BF16).astype(F32)
    rest = value - high
    middle = rest.astype(BF16).astype(F32)
    return [high, middle, rest - middle]


def stacked(parts, shape, axis):
    at = lax.broadcasted_iota(jnp.int32, shape, axis)
    out = jnp.zeros(shape, F32)
    for index, part in enumerate(parts):
        out = jnp.where(at == index, jnp.broadcast_to(part, shape), out)
    return out


def contract_last(a, b):
    return lax.dot_general(a, b, (((1,), (1,)), ((), ())), preferred_element_type=F32)


def merged(arrived):
    count = arrived.shape[0]
    wide = arrived.astype(F32)
    extra = wide[:, 8:16, :].reshape(count * 8, HD).astype(BF16)
    row = lax.broadcasted_iota(jnp.int32, (HD, 2 * HD), 0)
    col = lax.broadcasted_iota(jnp.int32, (HD, 2 * HD), 1)
    pick = jnp.where(row // 3 == col // HD, 1.0, 0.0).astype(BF16)
    spread = jnp.dot(extra, pick, preferred_element_type=F32)
    tops = spread[:, :HD].reshape(count, 8, HD)
    totals = spread[:, HD:].reshape(count, 8, HD)
    top = jnp.max(tops, axis=0)
    factor = jnp.exp2(tops - top[None])
    return top, jnp.sum(factor * totals, axis=0), jnp.sum(factor * wide[:, 0:8, :], axis=0)


def kernel(
    n_ctx,
    n_row,
    q_hbm,
    kv_hbm,
    suf_hbm,
    len_ref,
    idx_ref,
    down_hbm,
    up_hbm,
    att_ref,
    mix_ref,
    qv,
    qall,
    qown,
    sufv,
    sx,
    sr,
    kvb,
    vt,
    qb,
    sc,
    ob,
    rb,
    zs,
    zr,
    ad,
    ls,
    lr,
    s_q,
    s_suf,
    s_ad_loc,
    s_ad_send,
    s_ad_recv,
    s_a_send,
    s_a_recv,
    s_x_send,
    s_x_recv,
    s_kv_send,
    s_kv_recv,
    s_s_send,
    s_s_recv,
    s_o_send,
    s_o_recv,
    s_z_send,
    s_z_recv,
    s_l_send,
    s_l_recv,
):
    chips = n_ctx // 2
    pairs = chips // 2
    breadth = chips // COLUMN
    lanes = n_row * 8
    pd = kv_hbm.shape[1]
    sd = suf_hbm.shape[1]
    spos = sd // OWN
    scale = HD**-0.5 * math.log2(math.e)

    ctx = lax.axis_index("ctx")
    z = lax.axis_index("row")
    c = lax.rem(ctx, 2)
    chip = ctx // 2
    x = chip // COLUMN
    y = lax.rem(chip, COLUMN)
    g0 = chip // 2
    yl = lax.rem(chip, 2)
    sib = ctx + 1 - 2 * c

    q_copy = pltpu.make_async_copy(q_hbm, qv, s_q)
    q_copy.start()
    suf_copy = pltpu.make_async_copy(suf_hbm, sufv, s_suf)
    suf_copy.start()
    ad_loc = [
        pltpu.make_async_copy(down_hbm.at[0], ad.at[z, 0], s_ad_loc.at[0]),
        pltpu.make_async_copy(up_hbm.at[0], ad.at[z, 1], s_ad_loc.at[1]),
    ]
    for copy in ad_loc:
        copy.start()

    barrier = pltpu.get_barrier_semaphore()

    def greet_line(d, carry):
        pl.semaphore_signal(
            barrier, 1, device_id=(ctx, lax.rem(z + d, n_row)), device_id_type=MESH
        )
        return carry

    def greet_plane(d, carry):
        pl.semaphore_signal(
            barrier, 1, device_id=(lax.rem(ctx + d, n_ctx), z), device_id_type=MESH
        )
        return carry

    lax.fori_loop(1, n_row, greet_line, 0)
    lax.fori_loop(1, n_ctx, greet_plane, 0)

    q_copy.wait()
    queries = qv[...].astype(F32)
    for head in range(pairs * GROUP):
        qall[head * OWN : (head + 1) * OWN, :] = queries[:, head * HD : (head + 1) * HD]
    for side in range(2):
        start = pl.multiple_of(g0 * (GROUP * OWN) + side * VEC + 8 * c, 8)
        qown[side * 8 : (side + 1) * 8, :] = qall[pl.ds(start, 8), :]
    first = pl.ds(pl.multiple_of(z * VEC, VEC), VEC)
    qb[c, first, :] = qown[...].astype(BF16)

    pl.semaphore_wait(barrier, n_ctx - 1 + n_row - 1)

    def send_a(d, carry):
        pltpu.make_async_remote_copy(
            src_ref=qb.at[c, first],
            dst_ref=qb.at[c, first],
            send_sem=s_a_send,
            recv_sem=s_a_recv,
            device_id=(ctx, lax.rem(z + d, n_row)),
            device_id_type=MESH,
        ).start()
        return carry

    lax.fori_loop(1, n_row, send_a, 0)

    def place_kv(i, g):
        same = (g % 2) == y // 2
        target = (g // 2) * COLUMN + jnp.where(same, y, COLUMN - 1 - y)
        slot = 2 * x + jnp.where(same, 0, 1)
        columns = pl.ds(pl.multiple_of(g * HD, HD), HD)
        return target, slot, kv_hbm.at[i, :, columns]

    for i in range(2):

        def send_kv(d, carry):
            target, slot, part = place_kv(i, lax.rem(g0 + d, pairs))
            pltpu.make_async_remote_copy(
                src_ref=part,
                dst_ref=kvb.at[i, slot],
                send_sem=s_kv_send,
                recv_sem=s_kv_recv.at[i, slot],
                device_id=(target * 2 + c, z),
                device_id_type=MESH,
            ).start()
            return carry

        lax.fori_loop(1, pairs, send_kv, 0)
        _, slot, part = place_kv(i, g0)
        pltpu.make_async_copy(part, kvb.at[i, slot], s_kv_recv.at[i, slot]).start()

    for copy in ad_loc:
        copy.wait()

    def send_ad(d, carry):
        pltpu.make_async_remote_copy(
            src_ref=ad.at[z],
            dst_ref=ad.at[z],
            send_sem=s_ad_send,
            recv_sem=s_ad_recv,
            device_id=(ctx, lax.rem(z + d, n_row)),
            device_id_type=MESH,
        ).start()
        return carry

    lax.fori_loop(1, n_row, send_ad, 0)

    suf_copy.wait()
    at = lax.broadcasted_iota(jnp.int32, (GROUP * OWN, sd), 1)
    row = lax.broadcasted_iota(jnp.int32, (GROUP * OWN, sd), 0)
    owner = at // spos
    live = jnp.zeros((GROUP * OWN, sd), jnp.int32)
    for k in range(OWN):
        live = jnp.where(owner == k, len_ref[k], live)
    valid = (lax.rem(row, OWN) == owner) & (ctx * spos + lax.rem(at, spos) < live)
    for g in range(pairs):
        vectors = qall[g * GROUP * OWN : (g + 1) * GROUP * OWN, :].astype(BF16)
        scores = contract_last(vectors, sufv[0, :, g * HD : (g + 1) * HD]) * scale
        scores = jnp.where(valid, scores, -1e30)
        top = jnp.max(scores, axis=1, keepdims=True)
        weights = jnp.exp2(scores - top)
        total = jnp.sum(weights, axis=1, keepdims=True)
        out = jnp.dot(
            weights.astype(BF16),
            sufv[1, :, g * HD : (g + 1) * HD],
            preferred_element_type=F32,
        )
        extra = stacked(three(top) + three(total), (GROUP * OWN, HD), 1)
        sx[4 * g : 4 * g + 4] = jnp.concatenate(
            [out.reshape(4, 8, HD), extra.reshape(4, 8, HD)], axis=1
        ).astype(BF16)

    def send_s(d, carry):
        target = lax.rem(ctx + d, n_ctx)
        pltpu.make_async_remote_copy(
            src_ref=sx.at[target],
            dst_ref=sr.at[ctx],
            send_sem=s_s_send,
            recv_sem=s_s_recv,
            device_id=(target, z),
            device_id_type=MESH,
        ).start()
        return carry

    lax.fori_loop(1, n_ctx, send_s, 0)
    sr[ctx] = sx[ctx]

    def finish(k):
        part = ad.at[0 : n_row - 1]
        pltpu.make_async_copy(part, part, s_ad_send).wait()
        part = qb.at[0, 0 : (n_row - 1) * VEC]
        pltpu.make_async_copy(part, part, s_a_send).wait()
        part = kvb.at[:, 0 : pairs - 1]
        pltpu.make_async_copy(part, part, s_kv_send).wait()
        part = sx.at[0 : n_ctx - 1]
        pltpu.make_async_copy(part, part, s_s_send).wait()
        pltpu.make_async_copy(qb.at[0], qb.at[0], s_x_send).wait()
        part = ob.at[0:3]
        pltpu.make_async_copy(part, part, s_o_send).wait()
        part = zs.at[0 : n_row - 1]
        pltpu.make_async_copy(part, part, s_z_send).wait()
        part = lr.at[0 : n_ctx - 1]
        pltpu.make_async_copy(part, part, s_l_send).wait()

    part = qb.at[0, 0 : (n_row - 1) * VEC]
    pltpu.make_async_copy(part, part, s_a_recv).wait()
    exchange = pltpu.make_async_remote_copy(
        src_ref=qb.at[c],
        dst_ref=qb.at[c],
        send_sem=s_x_send,
        recv_sem=s_x_recv,
        device_id=(sib, z),
        device_id_type=MESH,
    )
    exchange.start()

    def vectors_of(core):
        wide = qb[core].astype(F32).reshape(n_row, 2, 8, HD)
        return jnp.concatenate(
            [wide[:, side].reshape(lanes, HD) for side in range(2)], axis=0
        ).astype(BF16)

    def chunk(j):
        return pl.multiple_of(2 * lax.rem(x + j, breadth), 2)

    def arrive(i, j):
        for side in range(2):
            slot = chunk(j) + side
            pltpu.make_async_copy(
                kvb.at[i, slot], kvb.at[i, slot], s_kv_recv.at[i, slot]
            ).wait()

    cores = (c, 1 - c)
    tops = []
    for h in range(2):
        if h == 1:
            exchange.wait_recv()
        vectors = vectors_of(cores[h])
        top = None
        for j in range(breadth):
            if h == 0:
                arrive(0, j)
            keys = kvb[0, pl.ds(chunk(j), 2)].reshape(2 * pd, HD)
            scores = contract_last(keys, vectors) * scale
            sc[h, j] = scores
            best = jnp.max(scores, axis=0, keepdims=True)
            top = best if top is None else jnp.maximum(top, best)
        tops.append(top)
    for j in range(breadth):
        arrive(1, j)
        vt[j] = kvb[1, pl.ds(chunk(j), 2)].reshape(2 * pd, HD).T

    for h in range(2):
        total = jnp.zeros((1, 2 * lanes), F32)
        acc = jnp.zeros((HD, 2 * lanes), F32)
        for j in range(breadth):
            weights = jnp.exp2(sc[h, j] - tops[h])
            total = total + jnp.sum(weights, axis=0, keepdims=True)
            acc = acc + jnp.dot(vt[j], weights.astype(BF16), preferred_element_type=F32)
        extra = stacked(three(tops[h]) + three(total), (EXTRA, 2 * lanes), 0)
        for side in range(2):
            target = (g0 * 2 + side) * 2 + cores[h]
            index = 2 * side + cores[h]
            columns = slice(side * lanes, (side + 1) * lanes)
            ob[index, 0:HD, :] = acc[:, columns].astype(BF16)
            ob[index, HD : HD + EXTRA, :] = extra[:, columns].astype(BF16)

            @pl.when(target != ctx)
            def _():
                pltpu.make_async_remote_copy(
                    src_ref=ob.at[index],
                    dst_ref=rb.at[2 * yl + c],
                    send_sem=s_o_send,
                    recv_sem=s_o_recv,
                    device_id=(target, z),
                    device_id_type=MESH,
                ).start()

            @pl.when(target == ctx)
            def _():
                pltpu.make_async_copy(ob.at[index], rb.at[2 * yl + c], s_o_recv).start()

    part = sr.at[0 : n_ctx - 1]
    pltpu.make_async_copy(part, part, s_s_recv).wait()
    near = merged(sr[...])

    pltpu.make_async_copy(rb, rb, s_o_recv).wait()
    tops, totals = [], []
    for k in range(4):
        extra = rb[k, HD : HD + EXTRA, :].astype(F32)
        tops.append(extra[0:1] + extra[1:2] + extra[2:3])
        totals.append(extra[3:4] + extra[4:5] + extra[5:6])
    top = functools.reduce(jnp.maximum, tops)
    acc = jnp.zeros((HD, lanes), F32)
    total = jnp.zeros((1, lanes), F32)
    for k in range(4):
        factor = jnp.exp2(tops[k] - top)
        acc = acc + factor * rb[k, 0:HD, :].astype(F32)
        total = total + factor * totals[k]
    extra = stacked(three(top) + three(total), (HD, lanes), 0)
    zs[...] = jnp.concatenate(
        [acc.T.reshape(n_row, 8, HD), extra.T.reshape(n_row, 8, HD)], axis=1
    ).astype(BF16)

    def send_z(d, carry):
        target = lax.rem(z + d, n_row)
        pltpu.make_async_remote_copy(
            src_ref=zs.at[target],
            dst_ref=zr.at[z],
            send_sem=s_z_send,
            recv_sem=s_z_recv,
            device_id=(ctx, target),
            device_id_type=MESH,
        ).start()
        return carry

    lax.fori_loop(1, n_row, send_z, 0)
    zr[z] = zs[z]

    pltpu.make_async_copy(ad.at[0 : n_row - 1], ad.at[0 : n_row - 1], s_ad_recv).wait()

    part = zr.at[0 : n_row - 1]
    pltpu.make_async_copy(part, part, s_z_recv).wait()
    far = merged(zr[...])
    top = jnp.maximum(near[0], far[0])
    parts = [jnp.exp2(near[0] - top), jnp.exp2(far[0] - top)]
    total = parts[0] * near[1] + parts[1] * far[1]
    acc = parts[0] * near[2] + parts[1] * far[2]
    attended = (acc / total).astype(BF16).astype(F32)
    attended = jnp.concatenate([attended[0:OWN], attended[OWN : 2 * OWN]], axis=1)
    att_ref[...] = attended.astype(BF16)

    rank = down_hbm.shape[1]
    width = n_row * rank // 2
    twice = jnp.concatenate([attended, attended], axis=0).astype(BF16)
    low = contract_last(twice, ad[:, 0].reshape(n_row * rank, 2 * HD))
    row = lax.broadcasted_iota(jnp.int32, (2 * OWN, width), 0)
    col = lax.broadcasted_iota(jnp.int32, (2 * OWN, width), 1)
    wanted = jnp.zeros((2 * OWN, width), jnp.int32)
    for k in range(OWN):
        wanted = jnp.where(lax.rem(row, OWN) == k, idx_ref[0, k], wanted)
    mine = wanted == col // rank + (n_row // 2) * (row // OWN)
    low = jnp.where(row < OWN, low[:, :width], low[:, width:])
    ls[...] = jnp.where(mine, low, 0.0)

    def send_l(d, carry):
        pltpu.make_async_remote_copy(
            src_ref=ls,
            dst_ref=lr.at[ctx],
            send_sem=s_l_send,
            recv_sem=s_l_recv,
            device_id=(lax.rem(ctx + d, n_ctx), z),
            device_id_type=MESH,
        ).start()
        return carry

    lax.fori_loop(1, n_ctx, send_l, 0)
    lr[ctx] = ls[...]
    pltpu.make_async_copy(lr.at[0 : n_ctx - 1], lr.at[0 : n_ctx - 1], s_l_recv).wait()
    low = jnp.sum(lr[...], axis=0).astype(BF16)
    up = ad[:, 1].reshape(n_row * rank, 2 * HD)
    first = jnp.dot(low, up[:width], preferred_element_type=F32)
    second = jnp.dot(low, up[width:], preferred_element_type=F32)
    delta = first[0:OWN] + second[OWN : 2 * OWN]
    mix_ref[...] = (attended + delta.astype(BF16).astype(F32)).astype(BF16)

    finish(99)


def body(n_ctx, n_row, queries, prefix, suffix, lengths, adapters, down, up):
    chips = n_ctx // 2
    pairs = chips // 2
    breadth = chips // COLUMN
    lanes = n_row * 8
    pd = prefix.shape[1]
    sd = suffix.shape[1] * suffix.shape[2]
    width = prefix.shape[2]
    rank = down.shape[2]
    suffix = suffix.reshape(2, sd, width)
    adapters = adapters.T
    down = jnp.transpose(down, (0, 2, 1))
    hbm = pl.BlockSpec(memory_space=pltpu.HBM)
    smem = pl.BlockSpec(memory_space=pltpu.SMEM)
    vmem = pl.BlockSpec(memory_space=pltpu.VMEM)
    dma = pltpu.SemaphoreType.DMA
    out = jax.ShapeDtypeStruct((OWN, 2 * HD), BF16)
    return pl.pallas_call(
        functools.partial(kernel, n_ctx, n_row),
        out_shape=(out, out),
        in_specs=[hbm, hbm, hbm, smem, smem, hbm, hbm],
        out_specs=(vmem, vmem),
        scratch_shapes=[
            pltpu.VMEM(queries.shape, BF16),
            pltpu.VMEM((pairs * GROUP * OWN, HD), F32),
            pltpu.VMEM((VEC, HD), F32),
            pltpu.VMEM(suffix.shape, BF16),
            pltpu.VMEM((n_ctx, 16, HD), BF16),
            pltpu.VMEM((n_ctx, 16, HD), BF16),
            pltpu.VMEM((2, 2 * breadth, pd, HD), BF16),
            pltpu.VMEM((breadth, HD, 2 * pd), BF16),
            pltpu.VMEM((2, n_row * VEC, HD), BF16),
            pltpu.VMEM((2, breadth, 2 * pd, 2 * lanes), F32),
            pltpu.VMEM((4, HD + EXTRA, lanes), BF16),
            pltpu.VMEM((4, HD + EXTRA, lanes), BF16),
            pltpu.VMEM((n_row, 16, HD), BF16),
            pltpu.VMEM((n_row, 16, HD), BF16),
            pltpu.VMEM((n_row, 2, rank, 2 * HD), BF16),
            pltpu.VMEM((2 * OWN, n_row * rank // 2), F32),
            pltpu.VMEM((n_ctx, 2 * OWN, n_row * rank // 2), F32),
            dma,
            dma,
            dma((2,)),
            dma,
            dma,
            dma,
            dma,
            dma,
            dma,
            dma,
            dma((2, 2 * breadth)),
            dma,
            dma,
            dma,
            dma,
            dma,
            dma,
            dma,
            dma,
        ],
        compiler_params=pltpu.CompilerParams(
            collective_id=0, has_side_effects=True, vmem_limit_bytes=64 * 1024 * 1024
        ),
        name="decode_attention",
    )(queries, prefix, suffix, lengths, adapters, down, up)


def solution(mesh):
    return jax.shard_map(
        functools.partial(body, mesh.shape["ctx"], mesh.shape["row"]),
        mesh=mesh,
        in_specs=(
            P("row", None),
            P(None, ("ctx", "row"), None),
            P(None, "row", "ctx", None),
            P("row"),
            P("row", None),
            P("row", "ctx", None),
            P("row", None, "ctx"),
        ),
        out_specs=(P("row", "ctx"), P("row", "ctx")),
        check_vma=False,
    )
```

time: 68.1 us -> 54.8 us (0.80)
  Pallas kernels: 60.1 us -> 52.1 us
  local copies, waits for them, and re-layouts: 6.96 us -> 1.89 us
    pallas_call x1, Pallas kernels: 60.1 us -> 52.1 us  [body(): pl.pallas_call(functools.partial(kernel, n_ctx, n_row), out_shape=(out, o...]
    unnamed x17 -> x6, local copies, waits for them, and re-layouts: 6.96 us -> 1.89 us
where the time goes in v2:
time: 54.8 us; the launch traced here: 54.6 us
  Pallas kernels  52.1 us (95%)
  local copies, waits for them, and re-layouts  1.89 us (3%)
  between operations  0.65 us (1%)
    pallas_call x1, Pallas kernels, body(): pl.pallas_call(functools.partial(kernel, n_ctx, n_row), out_shape=(out, o...  52.1 us
    unnamed x6, local copies, waits for them, and re-layouts  1.89 us

profile of v2, /device:TPU:1, one launch (start us, length us, event | category | flops | bytes accessed | tf_op | source)
XLA Modules:
  0.0 54.6 jit_solution(13989853457364247042)
XLA Ops:
  0.6 52.1 %decode_attention.1 = (bf16[4,256]{1,0:T(4,128)(2,1)}, bf16[4,256]{1,0:T(4,128)(2,1)}) custom-call(bf16[4,8192]{1,0:T(4,128)(2,1)} %q_hbm.1, bf16[2,256,1024]{2,1,0:T(8,128)(2,1)} %kv_hbm.1, bf16[2,128,1024]{2,1,0:T(8,128)(2,1)} %bitcast.3, s32[4]{0:T(128)} %len_ref.1, s32[1,4]{1,0:T(1,128)} %bitcast.5, bf16[1,16,256]{2,1,0:T(8,128)(2,1)} %bitcast.4, ...), custom_call_target="tpu_custom_call" | custom-call | tf_op jit(solution)/shard_map/decode_attention/pallas_call | solution.py:457
  52.7 0.0 copy-start.1
  52.7 0.7 %copy-done.1 = bf16[4,256]{1,0:T(4,128)(2,1)S(1)} copy-done((bf16[4,256]{1,0:T(4,128)(2,1)S(1)}, bf16[4,256]{1,0:T(4,128)(2,1)}, u32[]{:S(2)}) %copy-start.1) | copy-done | bytes 2072
  53.4 0.0 copy-start
  53.4 0.6 %copy.11 = bf16[4,256]{1,0:T(4,128)(2,1)} copy(bf16[4,256]{1,0:T(4,128)(2,1)S(1)} %copy-done.1) | data formatting | bytes 4096
  54.0 0.1 copy-done
  54.0 0.6 %copy.12 = bf16[4,256]{1,0:T(4,128)(2,1)} copy(bf16[4,256]{1,0:T(4,128)(2,1)S(1)} %copy-done) | data formatting | bytes 4096
Async XLA Ops:
  52.7 0.7 %copy-start.1 = (bf16[4,256]{1,0:T(4,128)(2,1)S(1)}, bf16[4,256]{1,0:T(4,128)(2,1)}, u32[]{:S(2)}) copy-start(bf16[4,256]{1,0:T(4,128)(2,1)} %get-tuple-element.4) | copy-start | bytes 6148
  53.4 0.7 %copy-start = (bf16[4,256]{1,0:T(4,128)(2,1)S(1)}, bf16[4,256]{1,0:T(4,128)(2,1)}, u32[]{:S(2)}) copy-start(bf16[4,256]{1,0:T(4,128)(2,1)} %get-tuple-element.5) | copy-start | bytes 6148

commit v3 on v2

--- a/solution.py
+++ b/solution.py
@@ -14,6 +14,7 @@
 VEC = 16
 EXTRA = 16
 COLUMN = 4
+NEAR = 4
 MESH = pl.DeviceIdType.MESH
 F32 = jnp.float32
 BF16 = jnp.bfloat16
@@ -63,8 +64,7 @@
     idx_ref,
     down_hbm,
     up_hbm,
-    att_ref,
-    mix_ref,
+    out_ref,
     qv,
     qall,
     qown,
@@ -80,6 +80,7 @@
     zs,
     zr,
     ad,
+    dt,
     ls,
     lr,
     s_q,
@@ -114,20 +115,26 @@
     ctx = lax.axis_index("ctx")
     z = lax.axis_index("row")
     c = lax.rem(ctx, 2)
+    groups = n_row // NEAR
+    zl = lax.rem(z, NEAR)
+    zh = z // NEAR
     chip = ctx // 2
     x = chip // COLUMN
     y = lax.rem(chip, COLUMN)
-    g0 = chip // 2
-    yl = lax.rem(chip, 2)
     sib = ctx + 1 - 2 * c
+
+    owns = y % 2 == x // 2
+    lead = jnp.where(owns, x, (x + 2) % COLUMN)
+    g0 = 2 * lead + jnp.where(owns, y, (y + 2) % COLUMN) // 2
+    seat = 2 * jnp.where(owns, 0, 1) + c
 
     q_copy = pltpu.make_async_copy(q_hbm, qv, s_q)
     q_copy.start()
     suf_copy = pltpu.make_async_copy(suf_hbm, sufv, s_suf)
     suf_copy.start()
     ad_loc = [
-        pltpu.make_async_copy(down_hbm.at[0], ad.at[z, 0], s_ad_loc.at[0]),
-        pltpu.make_async_copy(up_hbm.at[0], ad.at[z, 1], s_ad_loc.at[1]),
+        pltpu.make_async_copy(down_hbm.at[0], ad.at[zl, zh, 0], s_ad_loc.at[0]),
+        pltpu.make_async_copy(up_hbm.at[0], ad.at[zl, zh, 1], s_ad_loc.at[1]),
     ]
     for copy in ad_loc:
         copy.start()
@@ -175,11 +182,25 @@
     lax.fori_loop(1, n_row, send_a, 0)
 
     def place_kv(i, g):
-        same = (g % 2) == y // 2
-        target = (g // 2) * COLUMN + jnp.where(same, y, COLUMN - 1 - y)
-        slot = 2 * x + jnp.where(same, 0, 1)
+        home_x = g // 2
+        home_y = 2 * (g % 2) + g // 4
+        dx = (x - home_x + COLUMN) % COLUMN
+        dy = (y - home_y + COLUMN) % COLUMN
+        far = jnp.where(dx == 3, 1, dx) + jnp.where(dy == 3, 1, dy)
+        level = jnp.where(dx == dy, 1, jnp.where(dx == 2 * (g % 2), 1, 0))
+        level = jnp.where(jnp.logical_and(dx % 2 == 1, dx != dy), 0, level)
+        stay = jnp.where(far == 2, level, jnp.where(far < 2, 1, 0))
+        dx = (dx + 2 * (1 - stay)) % COLUMN
+        dy = (dy + 2 * (1 - stay)) % COLUMN
+        target_x = (home_x + 2 * (1 - stay)) % COLUMN
+        target_y = (home_y + 2 * (1 - stay)) % COLUMN
+        one = jnp.where(dy == 0, (dx + 1) // 2, jnp.where(dy == 1, 3, 4))
+        two = jnp.where(dx % 2 == 1, 5 + dx // 2, 7)
+        near = jnp.logical_or(dx % 2 == 0, dy % 2 == 0)
+        near = jnp.logical_and(near, jnp.logical_and(dx != 2, dy != 2))
+        slot = jnp.where(near, one, two)
         columns = pl.ds(pl.multiple_of(g * HD, HD), HD)
-        return target, slot, kv_hbm.at[i, :, columns]
+        return target_x * COLUMN + target_y, slot, kv_hbm.at[i, :, columns]
 
     for i in range(2):
 
@@ -198,22 +219,6 @@
         lax.fori_loop(1, pairs, send_kv, 0)
         _, slot, part = place_kv(i, g0)
         pltpu.make_async_copy(part, kvb.at[i, slot], s_kv_recv.at[i, slot]).start()
-
-    for copy in ad_loc:
-        copy.wait()
-
-    def send_ad(d, carry):
-        pltpu.make_async_remote_copy(
-            src_ref=ad.at[z],
-            dst_ref=ad.at[z],
-            send_sem=s_ad_send,
-            recv_sem=s_ad_recv,
-            device_id=(ctx, lax.rem(z + d, n_row)),
-            device_id_type=MESH,
-        ).start()
-        return carry
-
-    lax.fori_loop(1, n_row, send_ad, 0)
 
     suf_copy.wait()
     at = lax.broadcasted_iota(jnp.int32, (GROUP * OWN, sd), 1)
@@ -255,9 +260,44 @@
     lax.fori_loop(1, n_ctx, send_s, 0)
     sr[ctx] = sx[ctx]
 
+    for copy in ad_loc:
+        copy.wait()
+
+    def send_far(d, carry):
+        pltpu.make_async_remote_copy(
+            src_ref=ad.at[zl, zh],
+            dst_ref=ad.at[zl, zh],
+            send_sem=s_ad_send.at[0],
+            recv_sem=s_ad_recv.at[0],
+            device_id=(ctx, lax.rem(z + NEAR * d, n_row)),
+            device_id_type=MESH,
+        ).start()
+        return carry
+
+    lax.fori_loop(1, groups, send_far, 0)
+
+    def share_adapters():
+        part = ad.at[0, 0 : groups - 1]
+        pltpu.make_async_copy(part, part, s_ad_recv.at[0]).wait()
+        for d in (1, NEAR - 1, 2):
+            pltpu.make_async_remote_copy(
+                src_ref=ad.at[zl],
+                dst_ref=ad.at[zl],
+                send_sem=s_ad_send.at[1],
+                recv_sem=s_ad_recv.at[1],
+                device_id=(ctx, lax.rem(z + jnp.where(d < NEAR - 1, d, n_row - 1), n_row)),
+                device_id_type=MESH,
+            ).start()
+
+    def adapters_here():
+        part = ad.at[0 : NEAR - 1]
+        pltpu.make_async_copy(part, part, s_ad_recv.at[1]).wait()
+
     def finish(k):
-        part = ad.at[0 : n_row - 1]
-        pltpu.make_async_copy(part, part, s_ad_send).wait()
+        part = ad.at[0, 0 : groups - 1]
+        pltpu.make_async_copy(part, part, s_ad_send.at[0]).wait()
+        part = ad.at[0 : NEAR - 1]
+        pltpu.make_async_copy(part, part, s_ad_send.at[1]).wait()
         part = qb.at[0, 0 : (n_row - 1) * VEC]
         pltpu.make_async_copy(part, part, s_a_send).wait()
         part = kvb.at[:, 0 : pairs - 1]
@@ -266,7 +306,15 @@
         pltpu.make_async_copy(part, part, s_s_send).wait()
         pltpu.make_async_copy(qb.at[0], qb.at[0], s_x_send).wait()
         part = ob.at[0:3]
-        pltpu.make_async_copy(part, part, s_o_send).wait()
+
+        @pl.when(owns)
+        def _():
+            pltpu.make_async_copy(part, part, s_o_send).wait()
+
+        @pl.when(jnp.logical_not(owns))
+        def _():
+            pltpu.make_async_copy(ob, ob, s_o_send).wait()
+
         part = zs.at[0 : n_row - 1]
         pltpu.make_async_copy(part, part, s_z_send).wait()
         part = lr.at[0 : n_ctx - 1]
@@ -290,12 +338,9 @@
             [wide[:, side].reshape(lanes, HD) for side in range(2)], axis=0
         ).astype(BF16)
 
-    def chunk(j):
-        return pl.multiple_of(2 * lax.rem(x + j, breadth), 2)
-
     def arrive(i, j):
         for side in range(2):
-            slot = chunk(j) + side
+            slot = 2 * j + side
             pltpu.make_async_copy(
                 kvb.at[i, slot], kvb.at[i, slot], s_kv_recv.at[i, slot]
             ).wait()
@@ -310,7 +355,7 @@
         for j in range(breadth):
             if h == 0:
                 arrive(0, j)
-            keys = kvb[0, pl.ds(chunk(j), 2)].reshape(2 * pd, HD)
+            keys = kvb[0, 2 * j : 2 * j + 2].reshape(2 * pd, HD)
             scores = contract_last(keys, vectors) * scale
             sc[h, j] = scores
             best = jnp.max(scores, axis=0, keepdims=True)
@@ -318,7 +363,7 @@
         tops.append(top)
     for j in range(breadth):
         arrive(1, j)
-        vt[j] = kvb[1, pl.ds(chunk(j), 2)].reshape(2 * pd, HD).T
+        vt[j] = kvb[1, 2 * j : 2 * j + 2].reshape(2 * pd, HD).T
 
     for h in range(2):
         total = jnp.zeros((1, 2 * lanes), F32)
@@ -339,7 +384,7 @@
             def _():
                 pltpu.make_async_remote_copy(
                     src_ref=ob.at[index],
-                    dst_ref=rb.at[2 * yl + c],
+                    dst_ref=rb.at[seat],
                     send_sem=s_o_send,
                     recv_sem=s_o_recv,
                     device_id=(target, z),
@@ -348,11 +393,9 @@
 
             @pl.when(target == ctx)
             def _():
-                pltpu.make_async_copy(ob.at[index], rb.at[2 * yl + c], s_o_recv).start()
-
-    part = sr.at[0 : n_ctx - 1]
-    pltpu.make_async_copy(part, part, s_s_recv).wait()
-    near = merged(sr[...])
+                pltpu.make_async_copy(ob.at[index], rb.at[seat], s_o_recv).start()
+
+    share_adapters()
 
     pltpu.make_async_copy(rb, rb, s_o_recv).wait()
     tops, totals = [], []
@@ -387,7 +430,23 @@
     lax.fori_loop(1, n_row, send_z, 0)
     zr[z] = zs[z]
 
-    pltpu.make_async_copy(ad.at[0 : n_row - 1], ad.at[0 : n_row - 1], s_ad_recv).wait()
+    part = sr.at[0 : n_ctx - 1]
+    pltpu.make_async_copy(part, part, s_s_recv).wait()
+    near = merged(sr[...])
+
+    adapters_here()
+    rank = down_hbm.shape[1]
+    width = n_row * rank // 2
+    dt[...] = ad[:, :, 0].reshape(n_row * rank, 2 * HD).T
+    row = lax.broadcasted_iota(jnp.int32, (2 * OWN, width), 0)
+    col = lax.broadcasted_iota(jnp.int32, (2 * OWN, width), 1)
+    wanted = jnp.zeros((2 * OWN, width), jnp.int32)
+    for k in range(OWN):
+        adapter = idx_ref[0, k]
+        wanted = jnp.where(
+            lax.rem(row, OWN) == k, (adapter % NEAR) * groups + adapter // NEAR, wanted
+        )
+    mine = wanted == col // rank + (n_row // 2) * (row // OWN)
 
     part = zr.at[0 : n_row - 1]
     pltpu.make_async_copy(part, part, s_z_recv).wait()
@@ -398,18 +457,10 @@
     acc = parts[0] * near[2] + parts[1] * far[2]
     attended = (acc / total).astype(BF16).astype(F32)
     attended = jnp.concatenate([attended[0:OWN], attended[OWN : 2 * OWN]], axis=1)
-    att_ref[...] = attended.astype(BF16)
-
-    rank = down_hbm.shape[1]
-    width = n_row * rank // 2
+    out_ref[0] = attended.astype(BF16)
+
     twice = jnp.concatenate([attended, attended], axis=0).astype(BF16)
-    low = contract_last(twice, ad[:, 0].reshape(n_row * rank, 2 * HD))
-    row = lax.broadcasted_iota(jnp.int32, (2 * OWN, width), 0)
-    col = lax.broadcasted_iota(jnp.int32, (2 * OWN, width), 1)
-    wanted = jnp.zeros((2 * OWN, width), jnp.int32)
-    for k in range(OWN):
-        wanted = jnp.where(lax.rem(row, OWN) == k, idx_ref[0, k], wanted)
-    mine = wanted == col // rank + (n_row // 2) * (row // OWN)
+    low = jnp.dot(twice, dt[...], preferred_element_type=F32)
     low = jnp.where(row < OWN, low[:, :width], low[:, width:])
     ls[...] = jnp.where(mine, low, 0.0)
 
@@ -428,11 +479,11 @@
     lr[ctx] = ls[...]
     pltpu.make_async_copy(lr.at[0 : n_ctx - 1], lr.at[0 : n_ctx - 1], s_l_recv).wait()
     low = jnp.sum(lr[...], axis=0).astype(BF16)
-    up = ad[:, 1].reshape(n_row * rank, 2 * HD)
+    up = ad[:, :, 1].reshape(n_row * rank, 2 * HD)
     first = jnp.dot(low, up[:width], preferred_element_type=F32)
     second = jnp.dot(low, up[width:], preferred_element_type=F32)
     delta = first[0:OWN] + second[OWN : 2 * OWN]
-    mix_ref[...] = (attended + delta.astype(BF16).astype(F32)).astype(BF16)
+    out_ref[1] = (attended + delta.astype(BF16).astype(F32)).astype(BF16)
 
     finish(99)
 
@@ -453,12 +504,11 @@
     smem = pl.BlockSpec(memory_space=pltpu.SMEM)
     vmem = pl.BlockSpec(memory_space=pltpu.VMEM)
     dma = pltpu.SemaphoreType.DMA
-    out = jax.ShapeDtypeStruct((OWN, 2 * HD), BF16)
-    return pl.pallas_call(
+    both = pl.pallas_call(
         functools.partial(kernel, n_ctx, n_row),
-        out_shape=(out, out),
+        out_shape=jax.ShapeDtypeStruct((2, OWN, 2 * HD), BF16),
         in_specs=[hbm, hbm, hbm, smem, smem, hbm, hbm],
-        out_specs=(vmem, vmem),
+        out_specs=vmem,
         scratch_shapes=[
             pltpu.VMEM(queries.shape, BF16),
             pltpu.VMEM((pairs * GROUP * OWN, HD), F32),
@@ -474,14 +524,15 @@
             pltpu.VMEM((4, HD + EXTRA, lanes), BF16),
             pltpu.VMEM((n_row, 16, HD), BF16),
             pltpu.VMEM((n_row, 16, HD), BF16),
-            pltpu.VMEM((n_row, 2, rank, 2 * HD), BF16),
+            pltpu.VMEM((NEAR, n_row // NEAR, 2, rank, 2 * HD), BF16),
+            pltpu.VMEM((2 * HD, n_row * rank), BF16),
             pltpu.VMEM((2 * OWN, n_row * rank // 2), F32),
             pltpu.VMEM((n_ctx, 2 * OWN, n_row * rank // 2), F32),
             dma,
             dma,
             dma((2,)),
-            dma,
-            dma,
+            dma((2,)),
+            dma((2,)),
             dma,
             dma,
             dma,
@@ -502,6 +553,7 @@
         ),
         name="decode_attention",
     )(queries, prefix, suffix, lengths, adapters, down, up)
+    return both[0], both[1]
 
 
 def solution(mesh):

time: 54.8 us -> 52.1 us (0.951)
  Pallas kernels: 52.1 us -> 50.1 us
  local copies, waits for them, and re-layouts: 1.89 us -> 1.26 us
    pallas_call x1, Pallas kernels: 52.1 us -> 50.1 us  [body(): pl.pallas_call(functools.partial(kernel, n_ctx, n_row), out_shape=jax.Sha...]
    unnamed x6 -> x0, local copies, waits for them, and re-layouts: 1.89 us -> none
    squeeze x0 -> x1, local copies, waits for them, and re-layouts: none -> 1.26 us  [body(): return (both[0], both[1])]
where the time goes in v3:
time: 52.1 us; the launch traced here: 52 us
  Pallas kernels  50.1 us (96%)
  local copies, waits for them, and re-layouts  1.26 us (2%)
  between operations  0.64 us (1%)
    pallas_call x1, Pallas kernels, body(): pl.pallas_call(functools.partial(kernel, n_ctx, n_row), out_shape=jax.Sha...  50.1 us
    squeeze x1, local copies, waits for them, and re-layouts, body(): return (both[0], both[1])  1.26 us

profile of v3, /device:TPU:1, one launch (start us, length us, event | category | flops | bytes accessed | tf_op | source)
XLA Modules:
  0.0 52.0 jit_solution(6971304653372119024)
XLA Ops:
  0.6 50.1 %decode_attention.1 = bf16[2,4,256]{2,1,0:T(4,128)(2,1)} custom-call(bf16[4,8192]{1,0:T(4,128)(2,1)} %q_hbm.1, bf16[2,256,1024]{2,1,0:T(8,128)(2,1)} %kv_hbm.1, bf16[2,128,1024]{2,1,0:T(8,128)(2,1)} %bitcast.7, s32[4]{0:T(128)} %len_ref.1, s32[1,4]{1,0:T(1,128)} %bitcast.9, bf16[1,16,256]{2,1,0:T(8,128)(2,1)} %bitcast.8, bf16[1,16,256]{2,1,0:T(8,128)(2,1)} %up_hbm.1), custom_call_target="tpu_custom_call" | custom-call | tf_op jit(solution)/shard_map/decode_attention/pallas_call | solution.py:507
  50.7 1.3 %slice_bitcast_fusion = (bf16[4,256]{1,0:T(4,128)(2,1)}, bf16[4,256]{1,0:T(4,128)(2,1)}) fusion(bf16[2,4,256]{2,1,0:T(4,128)(2,1)} %decode_attention.1), kind=kLoop, calls=%fused_computation | loop fusion | bytes 8192 | tf_op jit(solution)/shard_map/squeeze | solution.py:556

commit v4 on v3

--- a/solution.py
+++ b/solution.py
@@ -60,11 +60,13 @@
     q_hbm,
     kv_hbm,
     suf_hbm,
-    len_ref,
-    idx_ref,
+    len_hbm,
+    idx_hbm,
     down_hbm,
     up_hbm,
     out_ref,
+    len_ref,
+    idx_ref,
     qv,
     qall,
     qown,
@@ -90,8 +92,6 @@
     s_ad_recv,
     s_a_send,
     s_a_recv,
-    s_x_send,
-    s_x_recv,
     s_kv_send,
     s_kv_recv,
     s_s_send,
@@ -128,6 +128,23 @@
     g0 = 2 * lead + jnp.where(owns, y, (y + 2) % COLUMN) // 2
     seat = 2 * jnp.where(owns, 0, 1) + c
 
+    barrier = pltpu.get_barrier_semaphore()
+
+    def greet_line(d, carry):
+        target = lax.rem(z + d + jnp.where(d < NEAR, n_row - NEAR, n_row - NEAR + 1), n_row)
+        for there in (ctx, sib):
+            pl.semaphore_signal(barrier, 1, device_id=(there, target), device_id_type=MESH)
+        return carry
+
+    def greet_plane(d, carry):
+        pl.semaphore_signal(
+            barrier, 1, device_id=(lax.rem(ctx + d, n_ctx), z), device_id_type=MESH
+        )
+        return carry
+
+    lax.fori_loop(0, 2 * NEAR, greet_line, 0)
+    lax.fori_loop(1, n_ctx, greet_plane, 0)
+
     q_copy = pltpu.make_async_copy(q_hbm, qv, s_q)
     q_copy.start()
     suf_copy = pltpu.make_async_copy(suf_hbm, sufv, s_suf)
@@ -136,25 +153,10 @@
         pltpu.make_async_copy(down_hbm.at[0], ad.at[zl, zh, 0], s_ad_loc.at[0]),
         pltpu.make_async_copy(up_hbm.at[0], ad.at[zl, zh, 1], s_ad_loc.at[1]),
     ]
+    ad_loc.append(pltpu.make_async_copy(len_hbm, len_ref, s_ad_loc.at[2]))
+    ad_loc.append(pltpu.make_async_copy(idx_hbm, idx_ref, s_ad_loc.at[3]))
     for copy in ad_loc:
         copy.start()
-
-    barrier = pltpu.get_barrier_semaphore()
-
-    def greet_line(d, carry):
-        pl.semaphore_signal(
-            barrier, 1, device_id=(ctx, lax.rem(z + d, n_row)), device_id_type=MESH
-        )
-        return carry
-
-    def greet_plane(d, carry):
-        pl.semaphore_signal(
-            barrier, 1, device_id=(lax.rem(ctx + d, n_ctx), z), device_id_type=MESH
-        )
-        return carry
-
-    lax.fori_loop(1, n_row, greet_line, 0)
-    lax.fori_loop(1, n_ctx, greet_plane, 0)
 
     q_copy.wait()
     queries = qv[...].astype(F32)
@@ -163,23 +165,31 @@
     for side in range(2):
         start = pl.multiple_of(g0 * (GROUP * OWN) + side * VEC + 8 * c, 8)
         qown[side * 8 : (side + 1) * 8, :] = qall[pl.ds(start, 8), :]
-    first = pl.ds(pl.multiple_of(z * VEC, VEC), VEC)
-    qb[c, first, :] = qown[...].astype(BF16)
-
-    pl.semaphore_wait(barrier, n_ctx - 1 + n_row - 1)
-
-    def send_a(d, carry):
+    qb[c, 0:VEC, :] = qown[...].astype(BF16)
+
+    pl.semaphore_wait(barrier, n_ctx - 1 + 4 * NEAR)
+
+    def send_q(first, count, place, there, step, sems):
         pltpu.make_async_remote_copy(
-            src_ref=qb.at[c, first],
-            dst_ref=qb.at[c, first],
-            send_sem=s_a_send,
-            recv_sem=s_a_recv,
-            device_id=(ctx, lax.rem(z + d, n_row)),
+            src_ref=qb.at[c, first * VEC : (first + count) * VEC],
+            dst_ref=qb.at[c, place * VEC : (place + count) * VEC],
+            send_sem=s_a_send.at[sems // 2],
+            recv_sem=s_a_recv.at[c, sems],
+            device_id=(there, lax.rem(z + step + n_row, n_row)),
             device_id_type=MESH,
         ).start()
-        return carry
-
-    lax.fori_loop(1, n_row, send_a, 0)
+
+    def wait_q(core, kind, count):
+        part = qb.at[0, 0 : count * VEC]
+        pltpu.make_async_copy(part, part, s_a_recv.at[core, kind]).wait()
+
+    for d in range(NEAR, 0, -1):
+        for there in (ctx, sib):
+            send_q(0, 1, n_row - d, there, d, 0)
+        if d < NEAR:
+            for there in (ctx, sib):
+                send_q(0, 1, d, there, -d, 1)
+    send_q(0, 1, 0, sib, 0, 1)
 
     def place_kv(i, g):
         home_x = g // 2
@@ -220,7 +230,16 @@
         _, slot, part = place_kv(i, g0)
         pltpu.make_async_copy(part, kvb.at[i, slot], s_kv_recv.at[i, slot]).start()
 
+    wait_q(c, 0, NEAR)
+    for there in (ctx, sib):
+        send_q(n_row - NEAR, NEAR, n_row - 2 * NEAR, there, NEAR, 2)
+    wait_q(c, 1, NEAR - 1)
+    for there in (ctx, sib):
+        send_q(0, NEAR, NEAR, there, -NEAR, 2)
+
     suf_copy.wait()
+    for copy in ad_loc:
+        copy.wait()
     at = lax.broadcasted_iota(jnp.int32, (GROUP * OWN, sd), 1)
     row = lax.broadcasted_iota(jnp.int32, (GROUP * OWN, sd), 0)
     owner = at // spos
@@ -260,9 +279,6 @@
     lax.fori_loop(1, n_ctx, send_s, 0)
     sr[ctx] = sx[ctx]
 
-    for copy in ad_loc:
-        copy.wait()
-
     def send_far(d, carry):
         pltpu.make_async_remote_copy(
             src_ref=ad.at[zl, zh],
@@ -274,7 +290,6 @@
         ).start()
         return carry
 
-    lax.fori_loop(1, groups, send_far, 0)
 
     def share_adapters():
         part = ad.at[0, 0 : groups - 1]
@@ -298,13 +313,14 @@
         pltpu.make_async_copy(part, part, s_ad_send.at[0]).wait()
         part = ad.at[0 : NEAR - 1]
         pltpu.make_async_copy(part, part, s_ad_send.at[1]).wait()
-        part = qb.at[0, 0 : (n_row - 1) * VEC]
-        pltpu.make_async_copy(part, part, s_a_send).wait()
+        part = qb.at[0, 0 : (4 * NEAR - 1) * VEC]
+        pltpu.make_async_copy(part, part, s_a_send.at[0]).wait()
+        part = qb.at[0, 0 : 4 * NEAR * VEC]
+        pltpu.make_async_copy(part, part, s_a_send.at[1]).wait()
         part = kvb.at[:, 0 : pairs - 1]
         pltpu.make_async_copy(part, part, s_kv_send).wait()
         part = sx.at[0 : n_ctx - 1]
         pltpu.make_async_copy(part, part, s_s_send).wait()
-        pltpu.make_async_copy(qb.at[0], qb.at[0], s_x_send).wait()
         part = ob.at[0:3]
 
         @pl.when(owns)
@@ -320,17 +336,8 @@
         part = lr.at[0 : n_ctx - 1]
         pltpu.make_async_copy(part, part, s_l_send).wait()
 
-    part = qb.at[0, 0 : (n_row - 1) * VEC]
-    pltpu.make_async_copy(part, part, s_a_recv).wait()
-    exchange = pltpu.make_async_remote_copy(
-        src_ref=qb.at[c],
-        dst_ref=qb.at[c],
-        send_sem=s_x_send,
-        recv_sem=s_x_recv,
-        device_id=(sib, z),
-        device_id_type=MESH,
-    )
-    exchange.start()
+    wait_q(c, 2, 2 * NEAR)
+    lax.fori_loop(1, groups, send_far, 0)
 
     def vectors_of(core):
         wide = qb[core].astype(F32).reshape(n_row, 2, 8, HD)
@@ -349,7 +356,9 @@
     tops = []
     for h in range(2):
         if h == 1:
-            exchange.wait_recv()
+            wait_q(1 - c, 0, NEAR)
+            wait_q(1 - c, 1, NEAR)
+            wait_q(1 - c, 2, 2 * NEAR)
         vectors = vectors_of(cores[h])
         top = None
         for j in range(breadth):
@@ -394,8 +403,6 @@
             @pl.when(target == ctx)
             def _():
                 pltpu.make_async_copy(ob.at[index], rb.at[seat], s_o_recv).start()
-
-    share_adapters()
 
     pltpu.make_async_copy(rb, rb, s_o_recv).wait()
     tops, totals = [], []
@@ -415,20 +422,21 @@
         [acc.T.reshape(n_row, 8, HD), extra.T.reshape(n_row, 8, HD)], axis=1
     ).astype(BF16)
 
-    def send_z(d, carry):
-        target = lax.rem(z + d, n_row)
+    def send_z(i, carry):
+        step = n_row // 2 + jnp.where(i % 2 == 0, -(i // 2), i // 2)
         pltpu.make_async_remote_copy(
-            src_ref=zs.at[target],
+            src_ref=zs.at[step],
             dst_ref=zr.at[z],
             send_sem=s_z_send,
             recv_sem=s_z_recv,
-            device_id=(ctx, target),
+            device_id=(ctx, lax.rem(z + step, n_row)),
             device_id_type=MESH,
         ).start()
         return carry
 
     lax.fori_loop(1, n_row, send_z, 0)
-    zr[z] = zs[z]
+    zr[z] = zs[0]
+    share_adapters()
 
     part = sr.at[0 : n_ctx - 1]
     pltpu.make_async_copy(part, part, s_s_recv).wait()
@@ -501,15 +509,16 @@
     adapters = adapters.T
     down = jnp.transpose(down, (0, 2, 1))
     hbm = pl.BlockSpec(memory_space=pltpu.HBM)
-    smem = pl.BlockSpec(memory_space=pltpu.SMEM)
     vmem = pl.BlockSpec(memory_space=pltpu.VMEM)
     dma = pltpu.SemaphoreType.DMA
     both = pl.pallas_call(
         functools.partial(kernel, n_ctx, n_row),
         out_shape=jax.ShapeDtypeStruct((2, OWN, 2 * HD), BF16),
-        in_specs=[hbm, hbm, hbm, smem, smem, hbm, hbm],
+        in_specs=[hbm] * 7,
         out_specs=vmem,
         scratch_shapes=[
+            pltpu.SMEM(lengths.shape, jnp.int32),
+            pltpu.SMEM(adapters.shape, jnp.int32),
             pltpu.VMEM(queries.shape, BF16),
             pltpu.VMEM((pairs * GROUP * OWN, HD), F32),
             pltpu.VMEM((VEC, HD), F32),
@@ -530,13 +539,11 @@
             pltpu.VMEM((n_ctx, 2 * OWN, n_row * rank // 2), F32),
             dma,
             dma,
+            dma((4,)),
             dma((2,)),
             dma((2,)),
             dma((2,)),
-            dma,
-            dma,
-            dma,
-            dma,
+            dma((2, 3)),
             dma,
             dma((2, 2 * breadth)),
             dma,

time: 52.1 us -> 51.5 us (0.988)
  Pallas kernels: 50.1 us -> 49.4 us
    pallas_call x1, Pallas kernels: 50.1 us -> 49.4 us  [body(): pl.pallas_call(functools.partial(kernel, n_ctx, n_row), out_shape=jax.Sha...]
where the time goes in v4:
time: 51.5 us; the launch traced here: 51.3 us
  Pallas kernels  49.4 us (96%)
  local copies, waits for them, and re-layouts  1.26 us (2%)
  between operations  0.64 us (1%)
    pallas_call x1, Pallas kernels, body(): pl.pallas_call(functools.partial(kernel, n_ctx, n_row), out_shape=jax.Sha...  49.4 us
    squeeze x1, local copies, waits for them, and re-layouts, body(): return (both[0], both[1])  1.26 us

profile of v4, /device:TPU:1, one launch (start us, length us, event | category | flops | bytes accessed | tf_op | source)
XLA Modules:
  0.0 51.3 jit_solution(17592866261476665397)
XLA Ops:
  0.6 49.4 %decode_attention.1 = bf16[2,4,256]{2,1,0:T(4,128)(2,1)} custom-call(bf16[4,8192]{1,0:T(4,128)(2,1)} %q_hbm.1, bf16[2,256,1024]{2,1,0:T(8,128)(2,1)} %kv_hbm.1, bf16[2,128,1024]{2,1,0:T(8,128)(2,1)} %bitcast.7, s32[4]{0:T(128)} %len_hbm.1, s32[1,4]{1,0:T(1,128)} %bitcast.9, bf16[1,16,256]{2,1,0:T(8,128)(2,1)} %bitcast.8, bf16[1,16,256]{2,1,0:T(8,128)(2,1)} %up_hbm.1), custom_call_target="tpu_custom_call" | custom-call | tf_op jit(solution)/shard_map/decode_attention/pallas_call | solution.py:514
  50.1 1.3 %slice_bitcast_fusion = (bf16[4,256]{1,0:T(4,128)(2,1)}, bf16[4,256]{1,0:T(4,128)(2,1)}) fusion(bf16[2,4,256]{2,1,0:T(4,128)(2,1)} %decode_attention.1), kind=kLoop, calls=%fused_computation | loop fusion | bytes 8192 | tf_op jit(solution)/shard_map/squeeze | solution.py:563

commit v5 on v4

--- a/solution.py
+++ b/solution.py
@@ -191,6 +191,39 @@
                 send_q(0, 1, d, there, -d, 1)
     send_q(0, 1, 0, sib, 0, 1)
 
+    def send_far(block, step, kind):
+        pltpu.make_async_remote_copy(
+            src_ref=ad.at[zl, block],
+            dst_ref=ad.at[zl, block],
+            send_sem=s_ad_send.at[kind],
+            recv_sem=s_ad_recv.at[kind],
+            device_id=(ctx, lax.rem(z + step + n_row, n_row)),
+            device_id_type=MESH,
+        ).start()
+
+    def pass_adapters():
+        part = ad.at[0, 0:2]
+        pltpu.make_async_copy(part, part, s_ad_recv.at[0]).wait()
+        send_far(lax.rem(zh + groups - 1, groups), NEAR, 1)
+
+    def share_adapters():
+        part = ad.at[0, 0]
+        pltpu.make_async_copy(part, part, s_ad_recv.at[1]).wait()
+        for d in (1, n_row - 1, 2):
+            pltpu.make_async_remote_copy(
+                src_ref=ad.at[zl],
+                dst_ref=ad.at[zl],
+                send_sem=s_ad_send.at[2],
+                recv_sem=s_ad_recv.at[2],
+                device_id=(ctx, lax.rem(z + d, n_row)),
+                device_id_type=MESH,
+            ).start()
+
+    for copy in ad_loc:
+        copy.wait()
+    send_far(zh, NEAR, 0)
+    send_far(zh, -NEAR, 0)
+
     def place_kv(i, g):
         home_x = g // 2
         home_y = 2 * (g % 2) + g // 4
@@ -238,8 +271,6 @@
         send_q(0, NEAR, NEAR, there, -NEAR, 2)
 
     suf_copy.wait()
-    for copy in ad_loc:
-        copy.wait()
     at = lax.broadcasted_iota(jnp.int32, (GROUP * OWN, sd), 1)
     row = lax.broadcasted_iota(jnp.int32, (GROUP * OWN, sd), 0)
     owner = at // spos
@@ -279,40 +310,17 @@
     lax.fori_loop(1, n_ctx, send_s, 0)
     sr[ctx] = sx[ctx]
 
-    def send_far(d, carry):
-        pltpu.make_async_remote_copy(
-            src_ref=ad.at[zl, zh],
-            dst_ref=ad.at[zl, zh],
-            send_sem=s_ad_send.at[0],
-            recv_sem=s_ad_recv.at[0],
-            device_id=(ctx, lax.rem(z + NEAR * d, n_row)),
-            device_id_type=MESH,
-        ).start()
-        return carry
-
-
-    def share_adapters():
-        part = ad.at[0, 0 : groups - 1]
-        pltpu.make_async_copy(part, part, s_ad_recv.at[0]).wait()
-        for d in (1, NEAR - 1, 2):
-            pltpu.make_async_remote_copy(
-                src_ref=ad.at[zl],
-                dst_ref=ad.at[zl],
-                send_sem=s_ad_send.at[1],
-                recv_sem=s_ad_recv.at[1],
-                device_id=(ctx, lax.rem(z + jnp.where(d < NEAR - 1, d, n_row - 1), n_row)),
-                device_id_type=MESH,
-            ).start()
-
     def adapters_here():
         part = ad.at[0 : NEAR - 1]
-        pltpu.make_async_copy(part, part, s_ad_recv.at[1]).wait()
+        pltpu.make_async_copy(part, part, s_ad_recv.at[2]).wait()
 
     def finish(k):
-        part = ad.at[0, 0 : groups - 1]
+        part = ad.at[0, 0:2]
         pltpu.make_async_copy(part, part, s_ad_send.at[0]).wait()
+        part = ad.at[0, 0]
+        pltpu.make_async_copy(part, part, s_ad_send.at[1]).wait()
         part = ad.at[0 : NEAR - 1]
-        pltpu.make_async_copy(part, part, s_ad_send.at[1]).wait()
+        pltpu.make_async_copy(part, part, s_ad_send.at[2]).wait()
         part = qb.at[0, 0 : (4 * NEAR - 1) * VEC]
         pltpu.make_async_copy(part, part, s_a_send.at[0]).wait()
         part = qb.at[0, 0 : 4 * NEAR * VEC]
@@ -337,7 +345,7 @@
         pltpu.make_async_copy(part, part, s_l_send).wait()
 
     wait_q(c, 2, 2 * NEAR)
-    lax.fori_loop(1, groups, send_far, 0)
+    pass_adapters()
 
     def vectors_of(core):
         wide = qb[core].astype(F32).reshape(n_row, 2, 8, HD)
@@ -404,6 +412,8 @@
             def _():
                 pltpu.make_async_copy(ob.at[index], rb.at[seat], s_o_recv).start()
 
+    share_adapters()
+
     pltpu.make_async_copy(rb, rb, s_o_recv).wait()
     tops, totals = [], []
     for k in range(4):
@@ -436,7 +446,6 @@
 
     lax.fori_loop(1, n_row, send_z, 0)
     zr[z] = zs[0]
-    share_adapters()
 
     part = sr.at[0 : n_ctx - 1]
     pltpu.make_async_copy(part, part, s_s_recv).wait()
@@ -455,6 +464,15 @@
             lax.rem(row, OWN) == k, (adapter % NEAR) * groups + adapter // NEAR, wanted
         )
     mine = wanted == col // rank + (n_row // 2) * (row // OWN)
+    seated = col // rank == lax.rem(row, OWN)
+
+    def fold(value):
+        shift = width // 2
+        while shift >= rank:
+            value = value + pltpu.roll(value, shift, 1)
+            shift //= 2
+        return value
+
 
     part = zr.at[0 : n_row - 1]
     pltpu.make_async_copy(part, part, s_z_recv).wait()
@@ -470,7 +488,8 @@
     twice = jnp.concatenate([attended, attended], axis=0).astype(BF16)
     low = jnp.dot(twice, dt[...], preferred_element_type=F32)
     low = jnp.where(row < OWN, low[:, :width], low[:, width:])
-    ls[...] = jnp.where(mine, low, 0.0)
+    low = fold(jnp.where(mine, low, 0.0))
+    ls[...] = jnp.sum(jnp.where(seated, low, 0.0), axis=0, keepdims=True)
 
     def send_l(d, carry):
         pltpu.make_async_remote_copy(
@@ -486,7 +505,8 @@
     lax.fori_loop(1, n_ctx, send_l, 0)
     lr[ctx] = ls[...]
     pltpu.make_async_copy(lr.at[0 : n_ctx - 1], lr.at[0 : n_ctx - 1], s_l_recv).wait()
-    low = jnp.sum(lr[...], axis=0).astype(BF16)
+    low = jnp.broadcast_to(jnp.sum(lr[...], axis=0), (2 * OWN, width))
+    low = jnp.where(mine, fold(jnp.where(seated, low, 0.0)), 0.0).astype(BF16)
     up = ad[:, :, 1].reshape(n_row * rank, 2 * HD)
     first = jnp.dot(low, up[:width], preferred_element_type=F32)
     second = jnp.dot(low, up[width:], preferred_element_type=F32)
@@ -535,13 +555,13 @@
             pltpu.VMEM((n_row, 16, HD), BF16),
             pltpu.VMEM((NEAR, n_row // NEAR, 2, rank, 2 * HD), BF16),
             pltpu.VMEM((2 * HD, n_row * rank), BF16),
-            pltpu.VMEM((2 * OWN, n_row * rank // 2), F32),
-            pltpu.VMEM((n_ctx, 2 * OWN, n_row * rank // 2), F32),
+            pltpu.VMEM((1, n_row * rank // 2), F32),
+            pltpu.VMEM((n_ctx, 1, n_row * rank // 2), F32),
             dma,
             dma,
             dma((4,)),
-            dma((2,)),
-            dma((2,)),
+            dma((3,)),
+            dma((3,)),
             dma((2,)),
             dma((2, 3)),
             dma,

time: 51.5 us -> 50.3 us (0.977)
  Pallas kernels: 49.4 us -> 48.3 us
    pallas_call x1, Pallas kernels: 49.4 us -> 48.3 us  [body(): pl.pallas_call(functools.partial(kernel, n_ctx, n_row), out_shape=jax.Sha...]
where the time goes in v5:
time: 50.3 us; the launch traced here: 50.2 us
  Pallas kernels  48.3 us (96%)
  local copies, waits for them, and re-layouts  1.26 us (3%)
  between operations  0.64 us (1%)
    pallas_call x1, Pallas kernels, body(): pl.pallas_call(functools.partial(kernel, n_ctx, n_row), out_shape=jax.Sha...  48.3 us
    squeeze x1, local copies, waits for them, and re-layouts, body(): return (both[0], both[1])  1.26 us

profile of v5, /device:TPU:1, one launch (start us, length us, event | category | flops | bytes accessed | tf_op | source)
XLA Modules:
  0.0 50.2 jit_solution(10411432789467744367)
XLA Ops:
  0.6 48.3 %decode_attention.1 = bf16[2,4,256]{2,1,0:T(4,128)(2,1)} custom-call(bf16[4,8192]{1,0:T(4,128)(2,1)} %q_hbm.1, bf16[2,256,1024]{2,1,0:T(8,128)(2,1)} %kv_hbm.1, bf16[2,128,1024]{2,1,0:T(8,128)(2,1)} %bitcast.7, s32[4]{0:T(128)} %len_hbm.1, s32[1,4]{1,0:T(1,128)} %bitcast.9, bf16[1,16,256]{2,1,0:T(8,128)(2,1)} %bitcast.8, bf16[1,16,256]{2,1,0:T(8,128)(2,1)} %up_hbm.1), custom_call_target="tpu_custom_call" | custom-call | tf_op jit(solution)/shard_map/decode_attention/pallas_call | solution.py:534
  48.9 1.3 %slice_bitcast_fusion = (bf16[4,256]{1,0:T(4,128)(2,1)}, bf16[4,256]{1,0:T(4,128)(2,1)}) fusion(bf16[2,4,256]{2,1,0:T(4,128)(2,1)} %decode_attention.1), kind=kLoop, calls=%fused_computation | loop fusion | bytes 8192 | tf_op jit(solution)/shard_map/squeeze | solution.py:583

commit v6 on v5

--- a/solution.py
+++ b/solution.py
@@ -128,6 +128,9 @@
     g0 = 2 * lead + jnp.where(owns, y, (y + 2) % COLUMN) // 2
     seat = 2 * jnp.where(owns, 0, 1) + c
 
+    def across(i, count):
+        return count // 2 + jnp.where(i % 2 == 0, -(i // 2), i // 2)
+
     barrier = pltpu.get_barrier_semaphore()
 
     def greet_line(d, carry):
@@ -138,7 +141,10 @@
 
     def greet_plane(d, carry):
         pl.semaphore_signal(
-            barrier, 1, device_id=(lax.rem(ctx + d, n_ctx), z), device_id_type=MESH
+            barrier,
+            1,
+            device_id=(lax.rem(ctx + across(d, n_ctx), n_ctx), z),
+            device_id_type=MESH,
         )
         return carry
 
@@ -295,21 +301,6 @@
             [out.reshape(4, 8, HD), extra.reshape(4, 8, HD)], axis=1
         ).astype(BF16)
 
-    def send_s(d, carry):
-        target = lax.rem(ctx + d, n_ctx)
-        pltpu.make_async_remote_copy(
-            src_ref=sx.at[target],
-            dst_ref=sr.at[ctx],
-            send_sem=s_s_send,
-            recv_sem=s_s_recv,
-            device_id=(target, z),
-            device_id_type=MESH,
-        ).start()
-        return carry
-
-    lax.fori_loop(1, n_ctx, send_s, 0)
-    sr[ctx] = sx[ctx]
-
     def adapters_here():
         part = ad.at[0 : NEAR - 1]
         pltpu.make_async_copy(part, part, s_ad_recv.at[2]).wait()
@@ -433,19 +424,35 @@
     ).astype(BF16)
 
     def send_z(i, carry):
-        step = n_row // 2 + jnp.where(i % 2 == 0, -(i // 2), i // 2)
+        target = i - 1 + jnp.where(i > z, 1, 0)
+        step = lax.rem(target - z + n_row, n_row)
         pltpu.make_async_remote_copy(
             src_ref=zs.at[step],
             dst_ref=zr.at[z],
             send_sem=s_z_send,
             recv_sem=s_z_recv,
-            device_id=(ctx, lax.rem(z + step, n_row)),
+            device_id=(ctx, target),
             device_id_type=MESH,
         ).start()
         return carry
 
     lax.fori_loop(1, n_row, send_z, 0)
     zr[z] = zs[0]
+    def send_s(d, carry):
+        target = lax.rem(ctx + d, n_ctx)
+        pltpu.make_async_remote_copy(
+            src_ref=sx.at[target],
+            dst_ref=sr.at[ctx],
+            send_sem=s_s_send,
+            recv_sem=s_s_recv,
+            device_id=(target, z),
+            device_id_type=MESH,
+        ).start()
+        return carry
+
+    lax.fori_loop(1, n_ctx, send_s, 0)
+    sr[ctx] = sx[ctx]
+
 
     part = sr.at[0 : n_ctx - 1]
     pltpu.make_async_copy(part, part, s_s_recv).wait()
@@ -497,7 +504,7 @@
             dst_ref=lr.at[ctx],
             send_sem=s_l_send,
             recv_sem=s_l_recv,
-            device_id=(lax.rem(ctx + d, n_ctx), z),
+            device_id=(lax.rem(ctx + across(d, n_ctx), n_ctx), z),
             device_id_type=MESH,
         ).start()
         return carry

time: 50.3 us -> 49.8 us (0.990)
  Pallas kernels: 48.3 us -> 47.7 us
    pallas_call x1, Pallas kernels: 48.3 us -> 47.7 us  [body(): pl.pallas_call(functools.partial(kernel, n_ctx, n_row), out_shape=jax.Sha...]
where the time goes in v6:
time: 49.8 us; the launch traced here: 49.6 us
  Pallas kernels  47.7 us (96%)
  local copies, waits for them, and re-layouts  1.26 us (3%)
  between operations  0.64 us (1%)
    pallas_call x1, Pallas kernels, body(): pl.pallas_call(functools.partial(kernel, n_ctx, n_row), out_shape=jax.Sha...  47.7 us
    squeeze x1, local copies, waits for them, and re-layouts, body(): return (both[0], both[1])  1.26 us

profile of v6, /device:TPU:1, one launch (start us, length us, event | category | flops | bytes accessed | tf_op | source)
XLA Modules:
  0.0 49.6 jit_solution(14233965892846298958)
XLA Ops:
  0.6 47.7 %decode_attention.1 = bf16[2,4,256]{2,1,0:T(4,128)(2,1)} custom-call(bf16[4,8192]{1,0:T(4,128)(2,1)} %q_hbm.1, bf16[2,256,1024]{2,1,0:T(8,128)(2,1)} %kv_hbm.1, bf16[2,128,1024]{2,1,0:T(8,128)(2,1)} %bitcast.7, s32[4]{0:T(128)} %len_hbm.1, s32[1,4]{1,0:T(1,128)} %bitcast.9, bf16[1,16,256]{2,1,0:T(8,128)(2,1)} %bitcast.8, bf16[1,16,256]{2,1,0:T(8,128)(2,1)} %up_hbm.1), custom_call_target="tpu_custom_call" | custom-call | tf_op jit(solution)/shard_map/decode_attention/pallas_call | solution.py:541
  48.3 1.3 %slice_bitcast_fusion = (bf16[4,256]{1,0:T(4,128)(2,1)}, bf16[4,256]{1,0:T(4,128)(2,1)}) fusion(bf16[2,4,256]{2,1,0:T(4,128)(2,1)} %decode_attention.1), kind=kLoop, calls=%fused_computation | loop fusion | bytes 8192 | tf_op jit(solution)/shard_map/squeeze | solution.py:590

commit v7 on v6

--- a/solution.py
+++ b/solution.py
@@ -148,8 +148,8 @@
         )
         return carry
 
+    lax.fori_loop(1, n_ctx, greet_plane, 0)
     lax.fori_loop(0, 2 * NEAR, greet_line, 0)
-    lax.fori_loop(1, n_ctx, greet_plane, 0)
 
     q_copy = pltpu.make_async_copy(q_hbm, qv, s_q)
     q_copy.start()
@@ -275,6 +275,8 @@
     wait_q(c, 1, NEAR - 1)
     for there in (ctx, sib):
         send_q(0, NEAR, NEAR, there, -NEAR, 2)
+
+    pass_adapters()
 
     suf_copy.wait()
     at = lax.broadcasted_iota(jnp.int32, (GROUP * OWN, sd), 1)
@@ -336,7 +338,6 @@
         pltpu.make_async_copy(part, part, s_l_send).wait()
 
     wait_q(c, 2, 2 * NEAR)
-    pass_adapters()
 
     def vectors_of(core):
         wide = qb[core].astype(F32).reshape(n_row, 2, 8, HD)
@@ -352,7 +353,6 @@
             ).wait()
 
     cores = (c, 1 - c)
-    tops = []
     for h in range(2):
         if h == 1:
             wait_q(1 - c, 0, NEAR)
@@ -368,19 +368,16 @@
             sc[h, j] = scores
             best = jnp.max(scores, axis=0, keepdims=True)
             top = best if top is None else jnp.maximum(top, best)
-        tops.append(top)
-    for j in range(breadth):
-        arrive(1, j)
-        vt[j] = kvb[1, 2 * j : 2 * j + 2].reshape(2 * pd, HD).T
-
-    for h in range(2):
         total = jnp.zeros((1, 2 * lanes), F32)
         acc = jnp.zeros((HD, 2 * lanes), F32)
         for j in range(breadth):
-            weights = jnp.exp2(sc[h, j] - tops[h])
+            if h == 0:
+                arrive(1, j)
+                vt[j] = kvb[1, 2 * j : 2 * j + 2].reshape(2 * pd, HD).T
+            weights = jnp.exp2(sc[h, j] - top)
             total = total + jnp.sum(weights, axis=0, keepdims=True)
             acc = acc + jnp.dot(vt[j], weights.astype(BF16), preferred_element_type=F32)
-        extra = stacked(three(tops[h]) + three(total), (EXTRA, 2 * lanes), 0)
+        extra = stacked(three(top) + three(total), (EXTRA, 2 * lanes), 0)
         for side in range(2):
             target = (g0 * 2 + side) * 2 + cores[h]
             index = 2 * side + cores[h]

time: 49.8 us -> 49.2 us (0.988)
  Pallas kernels: 47.7 us -> 47.1 us
    pallas_call x1, Pallas kernels: 47.7 us -> 47.1 us  [body(): pl.pallas_call(functools.partial(kernel, n_ctx, n_row), out_shape=jax.Sha...]
where the time goes in v7:
time: 49.2 us; the launch traced here: 49 us
  Pallas kernels  47.1 us (96%)
  local copies, waits for them, and re-layouts  1.26 us (3%)
  between operations  0.64 us (1%)
    pallas_call x1, Pallas kernels, body(): pl.pallas_call(functools.partial(kernel, n_ctx, n_row), out_shape=jax.Sha...  47.1 us
    squeeze x1, local copies, waits for them, and re-layouts, body(): return (both[0], both[1])  1.26 us

profile of v7, /device:TPU:1, one launch (start us, length us, event | category | flops | bytes accessed | tf_op | source)
XLA Modules:
  0.0 49.0 jit_solution(4763909684726363001)
XLA Ops:
  0.6 47.1 %decode_attention.1 = bf16[2,4,256]{2,1,0:T(4,128)(2,1)} custom-call(bf16[4,8192]{1,0:T(4,128)(2,1)} %q_hbm.1, bf16[2,256,1024]{2,1,0:T(8,128)(2,1)} %kv_hbm.1, bf16[2,128,1024]{2,1,0:T(8,128)(2,1)} %bitcast.7, s32[4]{0:T(128)} %len_hbm.1, s32[1,4]{1,0:T(1,128)} %bitcast.9, bf16[1,16,256]{2,1,0:T(8,128)(2,1)} %bitcast.8, bf16[1,16,256]{2,1,0:T(8,128)(2,1)} %up_hbm.1), custom_call_target="tpu_custom_call" | custom-call | tf_op jit(solution)/shard_map/decode_attention/pallas_call | solution.py:538
  47.7 1.3 %slice_bitcast_fusion = (bf16[4,256]{1,0:T(4,128)(2,1)}, bf16[4,256]{1,0:T(4,128)(2,1)}) fusion(bf16[2,4,256]{2,1,0:T(4,128)(2,1)} %decode_attention.1), kind=kLoop, calls=%fused_computation | loop fusion | bytes 8192 | tf_op jit(solution)/shard_map/squeeze | solution.py:587

commit v8 on v7

--- a/solution.py
+++ b/solution.py
@@ -251,8 +251,7 @@
         columns = pl.ds(pl.multiple_of(g * HD, HD), HD)
         return target_x * COLUMN + target_y, slot, kv_hbm.at[i, :, columns]
 
-    for i in range(2):
-
+    def send_cache(i):
         def send_kv(d, carry):
             target, slot, part = place_kv(i, lax.rem(g0 + d, pairs))
             pltpu.make_async_remote_copy(
@@ -269,6 +268,8 @@
         _, slot, part = place_kv(i, g0)
         pltpu.make_async_copy(part, kvb.at[i, slot], s_kv_recv.at[i, slot]).start()
 
+    send_cache(0)
+
     wait_q(c, 0, NEAR)
     for there in (ctx, sib):
         send_q(n_row - NEAR, NEAR, n_row - 2 * NEAR, there, NEAR, 2)
@@ -276,6 +277,7 @@
     for there in (ctx, sib):
         send_q(0, NEAR, NEAR, there, -NEAR, 2)
 
+    send_cache(1)
     pass_adapters()
 
     suf_copy.wait()

time: 49.2 us -> 49.1 us (level)
  no operation moved by 1% of the time
where the time goes in v8:
time: 49.1 us; the launch traced here: 48.9 us
  Pallas kernels  47 us (96%)
  local copies, waits for them, and re-layouts  1.26 us (3%)
  between operations  0.64 us (1%)
    pallas_call x1, Pallas kernels, body(): pl.pallas_call(functools.partial(kernel, n_ctx, n_row), out_shape=jax.Sha...  47 us
    squeeze x1, local copies, waits for them, and re-layouts, body(): return (both[0], both[1])  1.26 us

profile of v8, /device:TPU:1, one launch (start us, length us, event | category | flops | bytes accessed | tf_op | source)
XLA Modules:
  0.0 48.9 jit_solution(580943890569793642)
XLA Ops:
  0.6 47.0 %decode_attention.1 = bf16[2,4,256]{2,1,0:T(4,128)(2,1)} custom-call(bf16[4,8192]{1,0:T(4,128)(2,1)} %q_hbm.1, bf16[2,256,1024]{2,1,0:T(8,128)(2,1)} %kv_hbm.1, bf16[2,128,1024]{2,1,0:T(8,128)(2,1)} %bitcast.7, s32[4]{0:T(128)} %len_hbm.1, s32[1,4]{1,0:T(1,128)} %bitcast.9, bf16[1,16,256]{2,1,0:T(8,128)(2,1)} %bitcast.8, bf16[1,16,256]{2,1,0:T(8,128)(2,1)} %up_hbm.1), custom_call_target="tpu_custom_call" | custom-call | tf_op jit(solution)/shard_map/decode_attention/pallas_call | solution.py:540
  47.6 1.3 %slice_bitcast_fusion = (bf16[4,256]{1,0:T(4,128)(2,1)}, bf16[4,256]{1,0:T(4,128)(2,1)}) fusion(bf16[2,4,256]{2,1,0:T(4,128)(2,1)} %decode_attention.1), kind=kLoop, calls=%fused_computation | loop fusion | bytes 8192 | tf_op jit(solution)/shard_map/squeeze | solution.py:589
